TPU v7x, 32 devices: a whole 2x2x4 slice. The times are simulated.
32 devices in a mesh: section: 2 (over y), grp: 2 (over x), dp: 8 (over z, core).
Axes of the slice: x: 2, y: 2, z: 4, core: 2. Of those that a mesh axis runs over, the one named last changes fastest.
Arguments:
- embedded: bfloat16 [2, 16, 256, 768], P(None, ('grp', 'dp')), may hold values from -6 to 6
- lengths: int32 [2, 16], P(None, ('grp', 'dp')), may hold values from 64 to 256, as said below
- token_grads: bfloat16 [2, 16, 256, 768], P(None, ('grp', 'dp')), may hold values from -6 to 6
- score_grads: float32 [2, 16], P(None, ('grp', 'dp')), may hold values from -6 to 6
- w_qkv: bfloat16 [2, 768, 2304], P('section', 'dp'), may hold values from -0.21875 to 0.21875
- w_attn_out: bfloat16 [2, 768, 768], P('section', 'dp'), may hold values from -0.875 to 0.875
- w_up: bfloat16 [2, 768, 3072], P('section', 'dp'), may hold values from -0.21875 to 0.21875
- w_down: bfloat16 [2, 3072, 768], P('section', 'dp'), may hold values from -0.109375 to 0.109375
- biases: float32 [2, 7680], P('section'), may hold values from -1.5 to 1.5
- gains: float32 [2, 2, 768], P('section'), may hold values from 0.25 to 1.75
- head_weight: float32 [768], replicated, may hold values from -5 to 5
Outputs:
- section_out: bfloat16 [2, 2, 16, 256, 768], P('section', None, ('grp', 'dp'))
- grad_in: float32 [2, 2, 16, 256, 768], P('section', None, ('grp', 'dp'))
- grad_qkv: float32 [2, 768, 2304], P('section', 'dp')
- grad_attn_out: float32 [2, 768, 768], P('section', 'dp')
- grad_up: float32 [2, 768, 3072], P('section', 'dp')
- grad_down: float32 [2, 3072, 768], P('section', 'dp')
- grad_biases: float32 [2, 7680], P('section')
- grad_gains: float32 [2, 2, 768], P('section')
- grad_head: float32 [768], replicated
Inputs may be any that keep to these rules, and one draw needn't show every extreme that they name: `lengths`: token count of each pair; some pair has exactly 256.
All inputs are finite; a program needn't handle non-finite values.
Results may differ from a plain program's by a relative error of at most 0.023.
Values may be sent and summed in bfloat16 or wider, within the bound.
A program may use at most 192 MiB of HBM per device.

v0:
```python
import math

import jax
import jax.numpy as jnp
from jax import lax
from jax.sharding import PartitionSpec as P

D = 768
FF = 3072
HEADS = 12
HEAD = 64


EPSILON = 1e-06


def passed_along(x, axis, by):
    count = lax.axis_size(axis)
    pairs = [(i, i + by) for i in range(count) if 0 <= i + by < count]
    return lax.ppermute(x, axis, pairs)


def norm_rows(row_vals, gain_row, shift_row):
    row_mean = jnp.mean(row_vals, -1, keepdims=True)
    centred = row_vals - row_mean
    row_var = jnp.mean(centred * centred, -1, keepdims=True)
    return centred * lax.rsqrt(row_var + EPSILON) * gain_row + shift_row


def exact_gelu(inputs):
    return jax.nn.gelu(inputs, approximate=False)


def times_trans(left_rows, right_rows):
    return lax.dot_general(
        left_rows, right_rows, (((1,), (1,)), ((), ())), preferred_element_type=jnp.float32
    )


def cross_rows(left_rows, right_rows):
    return lax.dot_general(
        left_rows, right_rows, (((0,), (0,)), ((), ())), preferred_element_type=jnp.float32
    )


def split_bias(bias_row):
    bounds_list = [0, D, 2 * D, 3 * D, 3 * D + FF, 4 * D + FF, 5 * D + FF, 6 * D + FF]
    return [bias_row[bounds_list[piece_num] : bounds_list[piece_num + 1]] for piece_num in range(7)]


def head_split(qkv_low):
    seq_len = qkv_low.shape[0]
    return [
        qkv_low[:, part_num * D : (part_num + 1) * D].reshape(seq_len, HEADS, HEAD)
        for part_num in range(3)
    ]


def masked_scores(query_heads, key_heads, valid_mask):
    raw_scores = jnp.einsum(
        "qhd,khd->hqk", query_heads, key_heads, preferred_element_type=jnp.float32
    ) * (1.0 / math.sqrt(HEAD))
    return jnp.where(valid_mask[None, None, :], raw_scores, -1e30)


def layer_forward(hidden, valid_mask, weights, bias_row, gain_row):
    w_qkv, w_attn, w_up, w_down = weights
    q_bias, v_bias, o_bias, up_bias, down_bias, shift_one, shift_two = split_bias(bias_row)
    seq_len = hidden.shape[0]
    hidden_low = hidden.astype(jnp.bfloat16)
    joint_bias = jnp.concatenate([q_bias, jnp.zeros((D,), jnp.float32), v_bias])
    qkv_low = (jnp.dot(hidden_low, w_qkv, preferred_element_type=jnp.float32) + joint_bias).astype(
        jnp.bfloat16
    )
    query_heads, key_heads, value_heads = head_split(qkv_low)
    masked = masked_scores(query_heads, key_heads, valid_mask)
    row_top = jnp.max(masked, -1, keepdims=True)
    exp_scores = jnp.exp(masked - row_top)
    row_total = jnp.sum(exp_scores, -1, keepdims=True)
    prob_rows = exp_scores / row_total
    log_total = row_top + jnp.log(row_total)
    mixed_low = (
        jnp.einsum(
            "hqk,khd->qhd",
            prob_rows.astype(jnp.bfloat16),
            value_heads,
            preferred_element_type=jnp.float32,
        )
        .reshape(seq_len, D)
        .astype(jnp.bfloat16)
    )
    first_in = hidden + jnp.dot(mixed_low, w_attn, preferred_element_type=jnp.float32) + o_bias
    first_norm = norm_rows(first_in, gain_row[0], shift_one)
    first_low = first_norm.astype(jnp.bfloat16)
    inner_pre = jnp.dot(first_low, w_up, preferred_element_type=jnp.float32) + up_bias
    act_low = exact_gelu(inner_pre).astype(jnp.bfloat16)
    second_in = (
        first_norm + jnp.dot(act_low, w_down, preferred_element_type=jnp.float32) + down_bias
    )
    output = norm_rows(second_in, gain_row[1], shift_two)
    record = (
        hidden_low,
        qkv_low,
        log_total,
        mixed_low,
        first_in,
        first_low,
        inner_pre,
        act_low,
        second_in,
    )
    return (output, record)


def layer_backward(grad_out, record, valid_mask, weights, bias_row, gain_row):
    w_qkv, w_attn, w_up, w_down = weights
    (
        hidden_low,
        qkv_low,
        log_total,
        mixed_low,
        first_in,
        first_low,
        inner_pre,
        act_low,
        second_in,
    ) = record
    pieces = split_bias(bias_row)
    shift_one, shift_two = (pieces[5], pieces[6])
    seq_len = qkv_low.shape[0]
    norm_two = jax.vjp(norm_rows, second_in, gain_row[1], shift_two)[1]
    d_second, d_gain_two, d_shift_two = norm_two(grad_out)
    d_down_low = d_second.astype(jnp.bfloat16)
    d_act = times_trans(d_down_low, w_down)
    gelu_back = jax.vjp(exact_gelu, inner_pre)[1]
    d_inner_low = gelu_back(d_act)[0].astype(jnp.bfloat16)
    d_first = d_second + times_trans(d_inner_low, w_up)
    norm_one = jax.vjp(norm_rows, first_in, gain_row[0], shift_one)[1]
    d_first_in, d_gain_one, d_shift_one = norm_one(d_first)
    d_attn_low = d_first_in.astype(jnp.bfloat16)
    d_mixed_heads = (
        times_trans(d_attn_low, w_attn).astype(jnp.bfloat16).reshape(seq_len, HEADS, HEAD)
    )
    query_heads, key_heads, value_heads = head_split(qkv_low)
    prob_rows = jnp.exp(masked_scores(query_heads, key_heads, valid_mask) - log_total)
    d_probs = jnp.einsum(
        "qhd,khd->hqk", d_mixed_heads, value_heads, preferred_element_type=jnp.float32
    )
    d_scores_low = (prob_rows * (d_probs - jnp.sum(prob_rows * d_probs, -1, keepdims=True))).astype(
        jnp.bfloat16
    )
    scale_back = 1.0 / math.sqrt(HEAD)
    d_query = (
        jnp.einsum("hqk,khd->qhd", d_scores_low, key_heads, preferred_element_type=jnp.float32)
        * scale_back
    )
    d_key = (
        jnp.einsum("hqk,qhd->khd", d_scores_low, query_heads, preferred_element_type=jnp.float32)
        * scale_back
    )
    d_value = jnp.einsum(
        "hqk,qhd->khd",
        prob_rows.astype(jnp.bfloat16),
        d_mixed_heads,
        preferred_element_type=jnp.float32,
    )
    d_qkv_low = jnp.concatenate(
        [d_query.reshape(seq_len, D), d_key.reshape(seq_len, D), d_value.reshape(seq_len, D)], 1
    ).astype(jnp.bfloat16)
    d_hidden = d_first_in + times_trans(d_qkv_low, w_qkv)
    qkv_sums = jnp.sum(d_qkv_low.astype(jnp.float32), 0)
    bias_grad = jnp.concatenate(
        [
            qkv_sums[0:D],
            qkv_sums[2 * D : 3 * D],
            jnp.sum(d_attn_low.astype(jnp.float32), 0),
            jnp.sum(d_inner_low.astype(jnp.float32), 0),
            jnp.sum(d_down_low.astype(jnp.float32), 0),
            d_shift_one,
            d_shift_two,
        ]
    )
    gain_grad = jnp.stack([d_gain_one, d_gain_two])
    return (d_hidden, (d_qkv_low, d_attn_low, d_inner_low, d_down_low), bias_grad, gain_grad)


def section_forward(hidden, valid_mask, weight_list, biases, gains):
    hidden, record = layer_forward(hidden, valid_mask, weight_list[0], biases[0], gains[0])
    records = [record]
    return (
        hidden,
        tuple((jnp.stack([layer_rec[member] for layer_rec in records]) for member in range(9))),
    )


def section_backward(grad_rows, record, valid_mask, weight_list, biases, gains):
    layer_count = len(weight_list)
    part_lists = [None] * layer_count
    bias_lists = [None] * layer_count
    gain_lists = [None] * layer_count
    for layer_num in reversed(range(layer_count)):
        single = tuple((member[layer_num] for member in record))
        grad_rows, parts, bias_grad, gain_grad = layer_backward(
            grad_rows,
            single,
            valid_mask,
            weight_list[layer_num],
            biases[layer_num],
            gains[layer_num],
        )
        part_lists[layer_num] = parts
        bias_lists[layer_num] = bias_grad
        gain_lists[layer_num] = gain_grad
    stacked = tuple(
        (jnp.stack([layer_parts[member] for layer_parts in part_lists]) for member in range(4))
    )
    return (grad_rows, stacked, jnp.stack(bias_lists), jnp.stack(gain_lists))


def empty_forward(layer_count, seq_len):
    low_type, high_type = (jnp.bfloat16, jnp.float32)
    return (
        jnp.zeros((layer_count, seq_len, D), low_type),
        jnp.zeros((layer_count, seq_len, 3 * D), low_type),
        jnp.zeros((layer_count, HEADS, seq_len, 1), high_type),
        jnp.zeros((layer_count, seq_len, D), low_type),
        jnp.zeros((layer_count, seq_len, D), high_type),
        jnp.zeros((layer_count, seq_len, D), low_type),
        jnp.zeros((layer_count, seq_len, FF), high_type),
        jnp.zeros((layer_count, seq_len, FF), low_type),
        jnp.zeros((layer_count, seq_len, D), high_type),
    )


def empty_backward(layer_count, seq_len, bias_width):
    low_type = jnp.bfloat16
    parts = (
        jnp.zeros((layer_count, seq_len, 3 * D), low_type),
        jnp.zeros((layer_count, seq_len, D), low_type),
        jnp.zeros((layer_count, seq_len, FF), low_type),
        jnp.zeros((layer_count, seq_len, D), low_type),
    )
    return (
        jnp.zeros((seq_len, D), jnp.float32),
        parts,
        jnp.zeros((layer_count, bias_width), jnp.float32),
        jnp.zeros((layer_count, 2, D), jnp.float32),
    )


def on_device(
    embedded,
    lengths,
    token_grads,
    score_grads,
    w_qkv,
    w_attn_out,
    w_up,
    w_down,
    biases,
    gains,
    head_weight,
):
    section_index = lax.axis_index("section")
    section_count = lax.axis_size("section")
    micro_count = embedded.shape[0]
    seq_len = embedded.shape[2]
    layer_count = w_qkv.shape[0]
    bias_width = biases.shape[1]
    tick_count = micro_count + section_count - 1
    positions = jnp.arange(seq_len, dtype=jnp.int32)
    last_section = section_index == section_count - 1
    gathered = [
        (
            lax.all_gather(w_qkv[0], "dp", axis=0, tiled=True),
            lax.all_gather(w_attn_out[0], "dp", axis=0, tiled=True),
            lax.all_gather(w_up[0], "dp", axis=0, tiled=True),
            lax.all_gather(w_down[0], "dp", axis=0, tiled=True),
        )
    ]

    def run_forward(operands):
        return section_forward(operands[0], operands[1], gathered, biases, gains)

    def skip_forward(operands):
        return (jnp.zeros((seq_len, D), jnp.float32), empty_forward(layer_count, seq_len))

    incoming = jnp.zeros((seq_len, D), jnp.bfloat16)
    sent_list, head_rows, record_list = ([], [], [])
    for tick_num in range(tick_count):
        micro_num = tick_num - section_index
        active = (micro_num >= 0) & (micro_num < micro_count)
        safe_num = jnp.clip(micro_num, 0, micro_count - 1)
        own_input = lax.dynamic_index_in_dim(embedded[:, 0], safe_num, 0, False).astype(jnp.float32)
        section_input = jnp.where(section_index == 0, own_input, incoming.astype(jnp.float32))
        valid_mask = positions < lax.dynamic_index_in_dim(lengths[:, 0], safe_num, 0, False)
        section_output, record = lax.cond(
            active, run_forward, skip_forward, (section_input, valid_mask)
        )
        sent_rows = section_output.astype(jnp.bfloat16)
        sent_list.append(sent_rows)
        head_rows.append(section_output[0])
        record_list.append(record)
        if tick_num + 1 < tick_count:
            incoming = passed_along(sent_rows, "section", 1)
    forward_records = tuple(
        (jnp.stack([tick_rec[member] for tick_rec in record_list]) for member in range(9))
    )
    sent_all = jnp.stack(sent_list)
    section_out = jnp.stack(
        [
            lax.dynamic_index_in_dim(sent_all, micro_num + section_index, 0, False)
            for micro_num in range(micro_count)
        ]
    )[None, :, None]
    cls_all = jnp.stack(head_rows)

    def run_backward(operands):
        return section_backward(operands[0], operands[1], operands[2], gathered, biases, gains)

    def skip_backward(operands):
        return empty_backward(layer_count, seq_len, bias_width)

    incoming_grad = jnp.zeros((seq_len, D), jnp.bfloat16)
    grad_list, part_list = ([], [])
    bias_total = jnp.zeros((layer_count, bias_width), jnp.float32)
    gain_total = jnp.zeros((layer_count, 2, D), jnp.float32)
    head_total = jnp.zeros((D,), jnp.float32)
    for tick_num in range(tick_count):
        micro_num = tick_num - (section_count - 1 - section_index)
        active = (micro_num >= 0) & (micro_num < micro_count)
        safe_num = jnp.clip(micro_num, 0, micro_count - 1)
        valid_mask = positions < lax.dynamic_index_in_dim(lengths[:, 0], safe_num, 0, False)
        record = tuple(
            (
                lax.dynamic_index_in_dim(member, safe_num + section_index, 0, False)
                for member in forward_records
            )
        )
        token_cot = jnp.where(
            valid_mask[:, None],
            lax.dynamic_index_in_dim(token_grads[:, 0], safe_num, 0, False).astype(jnp.float32),
            0.0,
        )
        score_cot = lax.dynamic_index_in_dim(score_grads[:, 0], safe_num, 0, False)
        last_seed = token_cot.at[0].add(score_cot * head_weight)
        seed_grad = jnp.where(last_section, last_seed, incoming_grad.astype(jnp.float32))
        input_grad, parts, bias_grad, gain_grad = lax.cond(
            active, run_backward, skip_backward, (seed_grad, record, valid_mask)
        )
        cls_row = lax.dynamic_index_in_dim(cls_all, safe_num + section_index, 0, False)
        head_total = head_total + jnp.where(active & last_section, score_cot, 0.0) * cls_row
        bias_total = bias_total + bias_grad
        gain_total = gain_total + gain_grad
        grad_list.append(input_grad)
        part_list.append(parts)
        if tick_num + 1 < tick_count:
            incoming_grad = passed_along(input_grad.astype(jnp.bfloat16), "section", -1)
    grad_all = jnp.stack(grad_list)
    grad_in = jnp.stack(
        [
            lax.dynamic_index_in_dim(
                grad_all, micro_num + section_count - 1 - section_index, 0, False
            )
            for micro_num in range(micro_count)
        ]
    )[None, :, None]
    part_all = tuple(
        (jnp.stack([tick_parts[member] for tick_parts in part_list]) for member in range(4))
    )
    input_members = (0, 3, 5, 7)
    shard_lists = [[], [], [], []]
    terms = []
    for member in range(4):
        left_rows = jnp.concatenate(
            [
                lax.dynamic_index_in_dim(
                    forward_records[input_members[member]], micro_num + section_index, 0, False
                )[0]
                for micro_num in range(micro_count)
            ],
            0,
        )
        right_rows = jnp.concatenate(
            [
                lax.dynamic_index_in_dim(
                    part_all[member], micro_num + section_count - 1 - section_index, 0, False
                )[0]
                for micro_num in range(micro_count)
            ],
            0,
        )
        terms.append(cross_rows(left_rows, right_rows))
    local_rows = (
        lax.psum_scatter(
            terms[0].astype(jnp.bfloat16), "dp", scatter_dimension=0, tiled=True
        ).astype(jnp.float32),
        lax.psum_scatter(
            terms[1].astype(jnp.bfloat16), "dp", scatter_dimension=0, tiled=True
        ).astype(jnp.float32),
        lax.psum_scatter(
            terms[2].astype(jnp.bfloat16), "dp", scatter_dimension=0, tiled=True
        ).astype(jnp.float32),
        lax.psum_scatter(
            terms[3].astype(jnp.bfloat16), "dp", scatter_dimension=0, tiled=True
        ).astype(jnp.float32),
    )
    shards = (
        lax.psum(local_rows[0].astype(jnp.bfloat16), "grp").astype(jnp.float32),
        lax.psum(local_rows[1].astype(jnp.bfloat16), "grp").astype(jnp.float32),
        lax.psum(local_rows[2].astype(jnp.bfloat16), "grp").astype(jnp.float32),
        lax.psum(local_rows[3].astype(jnp.bfloat16), "grp").astype(jnp.float32),
    )
    for member in range(4):
        shard_lists[member].append(shards[member])
    all_layers = layer_count * section_count
    bias_place = lax.dynamic_update_slice(
        jnp.zeros((all_layers, bias_width), jnp.float32),
        bias_total,
        (section_index * layer_count, 0),
    )
    gain_place = lax.dynamic_update_slice(
        jnp.zeros((all_layers, 2, D), jnp.float32), gain_total, (section_index * layer_count, 0, 0)
    )
    bias_sum, gain_sum, head_sum = lax.psum(
        (bias_place, gain_place, head_total), ("section", "grp", "dp")
    )
    grad_biases = lax.dynamic_slice_in_dim(bias_sum, section_index * layer_count, layer_count, 0)
    grad_gains = lax.dynamic_slice_in_dim(gain_sum, section_index * layer_count, layer_count, 0)
    return (
        section_out,
        grad_in,
        jnp.stack(shard_lists[0]),
        jnp.stack(shard_lists[1]),
        jnp.stack(shard_lists[2]),
        jnp.stack(shard_lists[3]),
        grad_biases,
        grad_gains,
        head_sum,
    )


def solution(mesh):
    placed = (
        P(None, ("grp", "dp"), None, None),
        P(None, ("grp", "dp")),
        P(None, ("grp", "dp"), None, None),
        P(None, ("grp", "dp")),
        P("section", "dp", None),
        P("section", "dp", None),
        P("section", "dp", None),
        P("section", "dp", None),
        P("section", None),
        P("section", None, None),
        P(),
    )
    return jax.shard_map(
        on_device,
        mesh=mesh,
        in_specs=placed,
        out_specs=(
            P("section", None, ("grp", "dp"), None, None),
            P("section", None, ("grp", "dp"), None, None),
            P("section", "dp", None),
            P("section", "dp", None),
            P("section", "dp", None),
            P("section", "dp", None),
            P("section", None),
            P("section", None, None),
            P(),
        ),
        check_vma=False,
    )
```

profile of v0, /device:TPU:0, one launch (start us, length us, event | category | flops | bytes accessed | tf_op | source)
XLA Modules:
  0.0 947.4 jit_solution(4564800879766263550)
XLA Ops:
  13.4 21.6 %all-gather.11.cloned.1.call-done = bf16[1,768,768]{2,1,0:T(8,128)(2,1)} async-done(((bf16[1,96,768]{2,1,0:T(8,128)(2,1)}), bf16[1,768,768]{2,1,0:T(8,128)(2,1)}) %all-gather.11.cloned.1.call-update) | async-done | bytes 1179664 | tf_op jit(solution)/shard_map/all_gather | solution.py:276
  35.0 43.0 %all-gather.9.cloned.1.call-done = bf16[1,768,2304]{2,1,0:T(8,128)(2,1)} async-done(((bf16[1,96,2304]{2,1,0:T(8,128)(2,1)}), bf16[1,768,2304]{2,1,0:T(8,128)(2,1)}) %all-gather.9.cloned.1.call-update) | async-done | bytes 3538960 | tf_op jit(solution)/shard_map/all_gather | solution.py:275
  78.0 52.3 %all-gather.13.cloned.1.call-done = bf16[1,768,3072]{2,1,0:T(8,128)(2,1)} async-done(((bf16[1,96,3072]{2,1,0:T(8,128)(2,1)}), bf16[1,768,3072]{2,1,0:T(8,128)(2,1)}) %all-gather.13.cloned.1.call-update) | async-done | bytes 4718608 | tf_op jit(solution)/shard_map/all_gather | solution.py:277
  130.3 52.0 %all-gather.15.cloned.1.call-done = bf16[1,3072,768]{2,1,0:T(8,128)(2,1)} async-done(((bf16[1,384,768]{2,1,0:T(8,128)(2,1)}), bf16[1,3072,768]{2,1,0:T(8,128)(2,1)}) %all-gather.15.cloned.1.call-update) | async-done | bytes 4718608 | tf_op jit(solution)/shard_map/all_gather | solution.py:278
  182.3 37.4 %conditional.6 = (bf16[256,768]{1,0:T(8,128)(2,1)}, f32[1,768]{1,0:T(1,128)S(1)}, bf16[1,256,768]{2,1,0:T(8,128)(2,1)S(1)}, bf16[1,1,256,768]{3,2,1,0:T(8,128)(2...) conditional(s32[]{:T(128)} %convert_element_type.523, ...), branch_computations={%region_0.1_spmd, %region_1.8_spmd.clone} | conditional | flops 3894610176 | bytes 89536824 | solution.py:297
  198.8 10.3 %fusion.107 = (bf16[256,3072]{1,0:T(8,128)(2,1)}, f32[256,3072]{1,0:T(8,128)S(1)}) fusion(f32[3072]{0:T(1024)S(1)} %bitcast.725, bf16[768,3072]{1,0:T(8,128)(2,1)S(1)} %bitcast.733, f32[256,768]{1,0:T(8,128)} %get-tuple-element.1654, f32[768]{0:T(1024)S(1)} %get-tuple-element.1557, f32[768]{0:T(1024)S(1)} %get-tuple-element.1562, ...), kind=kOutput, calls=%fused_computation.288 | convolution fusion | flops 1260847104 | bytes 10244096 | tf_op jit(solution)/shard_map/cond/branch_1_fun/dot_general | solution.py:95
  232.6 49.2 %conditional.7 = (bf16[256,768]{1,0:T(8,128)(2,1)}, f32[1,768]{1,0:T(1,128)S(1)}, bf16[1,256,768]{2,1,0:T(8,128)(2,1)S(1)}, bf16[1,1,256,768]{3,2,1,0:T(8,128)(2...) conditional(s32[]{:T(128)} %convert_element_type.525, ...), branch_computations={%region_8.9_spmd, %region_9.16_spmd.clone.clone} | conditional | flops 3894806784 | bytes 99073640 | solution.py:297
  238.5 4.3 fusion.127
  261.4 10.5 %fusion.130 = (bf16[256,3072]{1,0:T(8,128)(2,1)S(1)}, f32[256,3072]{1,0:T(8,128)}) fusion(f32[3072]{0:T(1024)S(1)} %bitcast.723, bf16[768,3072]{1,0:T(8,128)(2,1)S(1)} %bitcast.735, f32[256,768]{1,0:T(8,128)} %get-tuple-element.1665, f32[768]{0:T(1024)S(1)} %copy-done.82, f32[768]{0:T(1024)S(1)} %get-tuple-element.1570, f32[256]{0:T(256)S(1)} %add_rsqrt_fusion.3, ...), kind=kOutput, calls=%fused_computation.347 | convolution fusion | flops 1260847104 | bytes 10244096 | tf_op jit(solution)/shard_map/cond/branch_1_fun/dot_general | solution.py:95
  281.8 4.6 collective-permute-start.1
  295.9 9.7 %conditional.8 = (f32[1,768]{1,0:T(1,128)S(1)}, bf16[1,256,768]{2,1,0:T(8,128)(2,1)}, bf16[1,1,256,768]{3,2,1,0:T(8,128)(2,1)}, f32[1,1,12,256,1]{3,2,4,1,0:T(8,...) conditional(s32[]{:T(128)} %convert_element_type.529, ...), branch_computations={%region_16.17_spmd, %region_17.24_spmd.clone.clone} | conditional | flops 3894806784 | bytes 88899104 | solution.py:297
  316.6 16.1 %conditional.9 = (f32[256,768]{1,0:T(8,128)}, f32[1,7680]{1,0:T(1,128)}, f32[1,2,768]{2,1,0:T(2,128)}, bf16[1,1,256,2304]{2,3,1,0:T(8,128)(2,1)}, bf16[1,1,256,7...) conditional(s32[]{:T(128)} %convert_element_type.533, () %tuple.203, ...), branch_computations={%region_24.25_spmd, %region_25.43_spmd} | conditional | flops 4215466240 | bytes 133183408 | solution.py:348
  338.1 92.2 %collective-permute-done.2 = bf16[256,768]{1,0:T(8,128)(2,1)} collective-permute-done((bf16[256,768]{1,0:T(8,128)(2,1)}, bf16[256,768]{1,0:T(8,128)(2,1)}, u32[]{:S(2)}, u32[]{:S(2)}) %collective-permute-start.2) | collective-permute-done | bytes 393248 | tf_op jit(solution)/shard_map/ppermute | solution.py:20
  433.2 56.9 %conditional.10 = (f32[256,768]{1,0:T(8,128)}, f32[1,7680]{1,0:T(1,128)}, f32[1,2,768]{2,1,0:T(2,128)}, bf16[1,1,256,2304]{2,3,1,0:T(8,128)(2,1)}, bf16[1,1,256,...) conditional(s32[]{:T(128)} %convert_element_type.534, ...), branch_computations={%region_43.44_spmd, %region_44.62_spmd} | conditional | flops 4215269632 | bytes 134580224 | solution.py:348
  455.6 12.1 %convert_reduce_fusion.4 = (f32[3072]{0:T(1024)}, bf16[256,3072]{1,0:T(8,128)(2,1)}) fusion(f32[3,1,256,3072]{3,2,1,0:T(8,128)} %get-tuple-element.1120, s32[]{:T(128)} %get-tuple-element.1119, bf16[256,768]{1,0:T(8,128)(2,1)} %get-tuple-element.1597, bf16[3072,768]{1,0:T(8,128)(2,1)} %get-tuple-element.1121), kind=kOutput, calls=%fused_computation.111 | convolution fusion | flops 1266152448 | bytes 9842692 | tf_op jit(solution)/shard_map/cond/branch_1_fun/dot_general | solution.py:35
  503.5 49.4 %conditional.11 = (f32[1,7680]{1,0:T(1,128)}, f32[1,2,768]{2,1,0:T(2,128)}, f32[1,256,768]{2,1,0:T(8,128)}, bf16[1,1,256,2304]{2,3,1,0:T(8,128)(2,1)}, bf16[1,1,...) conditional(s32[]{:T(128)} %convert_element_type.537, ...), branch_computations={%region_62.63_spmd, %region_63.81_spmd} | conditional | flops 4215269632 | bytes 123517744 | solution.py:348
  523.2 12.1 %convert_reduce_fusion.8 = (f32[3072]{0:T(1024)}, bf16[256,3072]{1,0:T(8,128)(2,1)}) fusion(f32[3,1,256,3072]{3,2,1,0:T(8,128)} %get-tuple-element.1144, s32[]{:T(128)} %get-tuple-element.1133, bf16[256,768]{1,0:T(8,128)(2,1)} %get-tuple-element.1608, bf16[3072,768]{1,0:T(8,128)(2,1)} %get-tuple-element.1145), kind=kOutput, calls=%fused_computation.204 | convolution fusion | flops 1266152448 | bytes 9842692 | tf_op jit(solution)/shard_map/cond/branch_1_fun/dot_general | solution.py:35
  576.2 4.3 convolution_convert_fusion.3
  587.4 4.4 convolution_convert_fusion.4
  597.3 36.7 %reduce-scatter.5.cloned.1.call-done = bf16[96,2304]{1,0:T(8,128)(2,1)} async-done(((bf16[768,2304]{1,0:T(8,128)(2,1)}), bf16[96,2304]{1,0:T(8,128)(2,1)}) %reduce-scatter.5.cloned.1.call-update) | async-done | bytes 442384 | tf_op jit(solution)/shard_map/reduce_scatter | solution.py:395
  634.0 55.9 %reduce-scatter.11.cloned.1.call-done = bf16[384,768]{1,0:T(8,128)(2,1)} async-done(((bf16[3072,768]{1,0:T(8,128)(2,1)}), bf16[384,768]{1,0:T(8,128)(2,1)}) %reduce-scatter.11.cloned.1.call-update) | async-done | bytes 589840 | tf_op jit(solution)/shard_map/reduce_scatter | solution.py:404
  689.9 55.8 %reduce-scatter.9.cloned.1.call-done = bf16[96,3072]{1,0:T(8,128)(2,1)} async-done(((bf16[768,3072]{1,0:T(8,128)(2,1)}), bf16[96,3072]{1,0:T(8,128)(2,1)}) %reduce-scatter.9.cloned.1.call-update) | async-done | bytes 589840 | tf_op jit(solution)/shard_map/reduce_scatter | solution.py:401
  750.8 121.4 %all-reduce.5.cloned.1.call-done = (f32[2,7680]{1,0:T(2,128)}, f32[2,2,768]{2,1,0:T(2,128)}, f32[768]{0:T(1024)}) async-done(((f32[2,7680]{1,0:T(2,128)}, f32[2,2,768]{2,1,0:T(2,128)}, f32[768]{0:T(1024)}), (f32[2,7680]{1,0:T(2,128)}, f32[2,2,768]{2,1,0:T(2,128)}, f32[768]{0:T(1024)})) %all-reduce.5.cloned.1.call-update) | async-done | bytes 76816 | tf_op jit(solution)/shard_map/psum | solution.py:425
  875.0 57.8 %all-reduce.7.cloned.1.call-done = (bf16[1,96,2304]{2,1,0:T(8,128)(2,1)}, bf16[1,96,768]{2,1,0:T(8,128)(2,1)}, bf16[1,96,3072]{2,1,0:T(8,128)(2,1)}, bf16[1,384,768]{2,1,0:T(8,128)(2,1)}) async-done(((bf16[1,96,2304]{2,1,0:T(8,128)(2,1)}, bf16[1,96,768]{2,1,0:T(8,128)(2,1)}, bf16[1,96,3072]{2,1,0:T(8,128)(2,1)}, bf16[1,384,768]{2,1,0:T(8,128)(2,1)}), (bf16[1,96,2304]{2,1,0:T(8,128)(2,1)}, ...) | async-done | bytes 1769488 | tf_op jit(solution)/shard_map/psum | solution.py:409
  (526 shorter events, 267.6 us)
Async XLA Ops:
  7.2 27.9 %all-gather.11.cloned.1.call-start = ((), (), s32[]{:S(2)}) async-start(), calls=%async_computation.9 | async-start | bytes 1327104 | tf_op jit(solution)/shard_map/all_gather | solution.py:276
  7.9 70.1 %all-gather.9.cloned.1.call-start = ((), (), s32[]{:S(2)}) async-start(), calls=%async_computation.8 | async-start | bytes 3981312 | tf_op jit(solution)/shard_map/all_gather | solution.py:275
  8.7 121.6 %all-gather.13.cloned.1.call-start = ((), (), s32[]{:S(2)}) async-start(), calls=%async_computation.10 | async-start | bytes 5308416 | tf_op jit(solution)/shard_map/all_gather | solution.py:277
  9.4 172.9 %all-gather.15.cloned.1.call-start = ((), (), s32[]{:S(2)}) async-start(), calls=%async_computation.11 | async-start | bytes 5308416 | tf_op jit(solution)/shard_map/all_gather | solution.py:278
  10.0 587.3 %reduce-scatter.7.cloned.1.call-start = ((), (), s32[]{:S(2)}) async-start(), calls=%async_computation.5 | async-start | bytes 1327104 | tf_op jit(solution)/shard_map/reduce_scatter | solution.py:398
  195.3 13.8 %copy-start.25 = (bf16[12,64,256]{2,1,0:T(8,128)(2,1)}, bf16[12,64,256]{2,1,0:T(8,128)(2,1)S(1)}, u32[]{:S(2)}) copy-start(bf16[12,64,256]{2,1,0:T(8,128)(2,1)S(1)} %fusion.120) | copy-start | bytes 1179652 | tf_op jit(solution)/shard_map/cond
  220.3 10.6 %collective-permute-start = (bf16[256,768]{1,0:T(8,128)(2,1)}, bf16[256,768]{1,0:T(8,128)(2,1)S(1)}, u32[]{:S(2)}, u32[]{:S(2)}) collective-permute-start(bf16[256,768]{1,0:T(8,128)(2,1)} %get-tuple-element.1216), channel_id=1, source_target_pairs={{0,16},{1,17},{2,18},{3,19},{4,20},{5,21},{6,22},{7,23},{8,24},{9,... | collective-permute-start | bytes 1179656 | tf_op jit(solution)/shard_map/ppermute | solution.py:20
  257.7 14.2 %copy-start.26 = (bf16[12,64,256]{2,1,0:T(8,128)(2,1)}, bf16[12,64,256]{2,1,0:T(8,128)(2,1)S(1)}, u32[]{:S(2)}) copy-start(bf16[12,64,256]{2,1,0:T(8,128)(2,1)S(1)} %fusion.143) | copy-start | bytes 1179652 | tf_op jit(solution)/shard_map/cond
  258.4 13.5 %slice-start.14 = ((s8[4718592]{0:T(1024)(128)(4,1)}), s8[4194304]{0:T(1024)(128)(4,1)S(1)}, s32[]{:S(2)}) async-start(s8[4718592]{0:T(1024)(128)(4,1)} %bitcast.752), calls=%async_computation.28 | async-start | bytes 8388608 | tf_op jit(solution)/shard_map/cond
  281.8 13.1 %collective-permute-start.1 = (bf16[256,768]{1,0:T(8,128)(2,1)}, bf16[256,768]{1,0:T(8,128)(2,1)S(1)}, u32[]{:S(2)}, u32[]{:S(2)}) collective-permute-start(bf16[256,768]{1,0:T(8,128)(2,1)} %get-tuple-element.1218), channel_id=1, source_target_pairs={{0,16},{1,17},{2,18},{3,19},{4,20},{5,21},{6,22},{7,23},{8,24},{9,... | collective-permute-start | bytes 1179656 | tf_op jit(solution)/shard_map/ppermute | solution.py:20
  334.7 95.6 %collective-permute-start.2 = (bf16[256,768]{1,0:T(8,128)(2,1)}, bf16[256,768]{1,0:T(8,128)(2,1)}, u32[]{:S(2)}, u32[]{:S(2)}) collective-permute-start(bf16[256,768]{1,0:T(8,128)(2,1)} %convert_element_type.535), channel_id=1, source_target_pairs={{16,0},{17,1},{18,2},{19,3},{20,4},{21,5},{22,6},{23,7},{24,8},{25... | collective-permute-start | bytes 1179656 | tf_op jit(solution)/shard_map/ppermute | solution.py:20
  336.0 96.3 %copy-start.37 = (bf16[2,1,256,768]{3,2,1,0:T(8,128)(2,1)S(1)}, bf16[2,1,256,768]{3,2,1,0:T(8,128)(2,1)}, u32[]{:S(2)}) copy-start(bf16[2,1,256,768]{3,2,1,0:T(8,128)(2,1)} %param.31) | copy-start | bytes 2359300
  338.1 94.2 %copy-start.48 = (bf16[3,1,256,768]{2,3,1,0:T(8,128)(2,1)}, bf16[3,1,256,768]{2,3,1,0:T(8,128)(2,1)S(1)}, u32[]{:S(2)}) copy-start(bf16[3,1,256,768]{2,3,1,0:T(8,128)(2,1)S(1)} %constant_dynamic-update-slice_fusion.40) | copy-start | bytes 3538948
  452.8 14.9 %slice-start.8 = ((s8[4718592]{0:T(1024)(128)(4,1)}), s8[4194304]{0:T(1024)(128)(4,1)S(1)}, s32[]{:S(2)}) async-start(s8[4718592]{0:T(1024)(128)(4,1)} %bitcast.740), calls=%async_computation.22 | async-start | bytes 8388608 | tf_op jit(solution)/shard_map/cond
  490.0 13.4 %copy-start.38 = (bf16[2,1,256,768]{3,2,1,0:T(8,128)(2,1)S(1)}, bf16[2,1,256,768]{3,2,1,0:T(8,128)(2,1)}, u32[]{:S(2)}) copy-start(bf16[2,1,256,768]{3,2,1,0:T(8,128)(2,1)} %param.31) | copy-start | bytes 2359300
  490.0 13.4 %copy-start.138 = (s32[2,1]{0,1:T(1,128)S(1)}, s32[2,1]{0,1:T(1,128)}, u32[]{:S(2)}) copy-start(s32[2,1]{0,1:T(1,128)} %param.30) | copy-start | bytes 28
  491.3 11.1 %collective-permute-start.3 = (bf16[256,768]{1,0:T(8,128)(2,1)S(1)}, bf16[256,768]{1,0:T(8,128)(2,1)S(1)}, u32[]{:S(2)}, u32[]{:S(2)}) collective-permute-start(bf16[256,768]{1,0:T(8,128)(2,1)S(1)} %convert_element_type.538), channel_id=1, source_target_pairs={{16,0},{17,1},{18,2},{19,3},{20,4},{21,5},{22,6},{23,7},{24,8},{25... | collective-permute-start | bytes 1179656 | tf_op jit(solution)/shard_map/ppermute | solution.py:20
  520.4 14.9 %slice-start.10 = ((s8[4718592]{0:T(1024)(128)(4,1)}), s8[4194304]{0:T(1024)(128)(4,1)S(1)}, s32[]{:S(2)}) async-start(s8[4718592]{0:T(1024)(128)(4,1)} %bitcast.742), calls=%async_computation.24 | async-start | bytes 8388608 | tf_op jit(solution)/shard_map/cond
  558.9 75.1 %reduce-scatter.5.cloned.1.call-start = ((), (), s32[]{:S(2)}) async-start(), calls=%async_computation.4 | async-start | bytes 3981312 | tf_op jit(solution)/shard_map/reduce_scatter | solution.py:395
  569.3 120.6 %reduce-scatter.11.cloned.1.call-start = ((), (), s32[]{:S(2)}) async-start(), calls=%async_computation.7 | async-start | bytes 5308416 | tf_op jit(solution)/shard_map/reduce_scatter | solution.py:404
  580.5 165.1 %reduce-scatter.9.cloned.1.call-start = ((), (), s32[]{:S(2)}) async-start(), calls=%async_computation.6 | async-start | bytes 5308416 | tf_op jit(solution)/shard_map/reduce_scatter | solution.py:401
  591.9 280.3 %all-reduce.5.cloned.1.call-start = ((), (), s32[]{:S(2)}) async-start(), calls=%async_computation.12 | async-start | bytes 155648 | tf_op jit(solution)/shard_map/psum | solution.py:425
  597.2 335.6 %all-reduce.7.cloned.1.call-start = ((), (), s32[]{:S(2)}) async-start(), calls=%async_computation.13 | async-start | bytes 3538944 | tf_op jit(solution)/shard_map/psum | solution.py:409
  872.2 67.5 %copy-start.117 = (f32[768]{0:T(1024)S(1)}, f32[768]{0:T(1024)}, u32[]{:S(2)}) copy-start(f32[768]{0:T(1024)} %get-tuple-element.1828) | copy-start | bytes 9220
  (104 other events, 498.6 us)
Sparse Core Ops, SparseCore 0:
  9.7 25.3 all-gather.10
  36.7 41.2 all-gather.8
  79.6 50.5 all-gather.12
  131.8 50.5 all-gather.14
  559.0 30.5 reduce-scatter.6
  591.8 42.1 reduce-scatter.4
  636.4 53.4 reduce-scatter.10
  692.3 53.3 reduce-scatter.8
  753.8 118.4 all-reduce.4
  874.7 58.0 all-reduce.6
where the time goes:
time: 960 us; the launch traced here: 947 us
  waiting for transfers between devices  598 us (62%)
  local copies, waits for them, and re-layouts  122 us (13%)
  matrix products  108 us (11%)
  other arithmetic  81.4 us (8%)
  between operations  16.9 us (2%)
  loops' own time  11.7 us (1%)
  starting transfers between devices  9.71 us (1%)
    psum x1, waiting for transfers between devices, on_device(): lax.psum((bias_place, gain_place, head_total), ('section', 'grp', 'dp'))  121 us
    ppermute x4, waiting for transfers between devices, passed_along(): return lax.ppermute(x, axis, pairs)  98.8 us
    psum x1, waiting for transfers between devices, on_device(): lax.psum(local_rows[0].astype(jnp.bfloat16), 'grp').astype(jnp.float32)  57.8 us
    reduce_scatter x1, waiting for transfers between devices, on_device(): lax.psum_scatter(terms[3].astype(jnp.bfloat16), 'dp', scatter_dimension=0...  55.9 us
    reduce_scatter x1, waiting for transfers between devices, on_device(): lax.psum_scatter(terms[2].astype(jnp.bfloat16), 'dp', scatter_dimension=0...  55.8 us
    all_gather x1, waiting for transfers between devices, on_device(): lax.all_gather(w_up[0], 'dp', axis=0, tiled=True)  52.3 us
    all_gather x1, waiting for transfers between devices, on_device(): lax.all_gather(w_down[0], 'dp', axis=0, tiled=True)  52 us
    all_gather x1, waiting for transfers between devices, on_device(): lax.all_gather(w_qkv[0], 'dp', axis=0, tiled=True)  43 us
  transfers between devices with their start and end apart: 14, of which 13 were waited for; matrix products, arithmetic and copies ran while one was open for 7% of the time, Pallas kernels for 0%

commit v1 on v0

v1 whole, which is shorter than its diff:
```python
import functools
import math

import jax
import jax.numpy as jnp
from jax import lax
from jax.experimental import pallas as pl
from jax.experimental.pallas import tpu as pltpu
from jax.sharding import PartitionSpec as P

D = 768
FF = 3072
HEADS = 12
HEAD = 64
EPSILON = 1e-06
CHUNKS = 12
HALF = D // 2
DOWN = 8 * D
DOWN_GRAD = 12 * D
SCALE = 1.0 / math.sqrt(HEAD)
F32 = jnp.float32
BF = jnp.bfloat16
MESH = pl.DeviceIdType.MESH
BQ, BV, BO, BU, BD, BETA1, BETA2, GAIN1, GAIN2, HEAD_ROW = 0, 1, 2, 3, 7, 8, 9, 10, 11, 12
SMALL = 16


def dot(a, b):
    return lax.dot_general(a, b, (((1,), (0,)), ((), ())), preferred_element_type=F32)


def dot_t(a, b):
    return lax.dot_general(a, b, (((1,), (1,)), ((), ())), preferred_element_type=F32)


def dot_c(a, b):
    return lax.dot_general(a, b, (((0,), (0,)), ((), ())), preferred_element_type=F32)


def span(i, width):
    return pl.ds(pl.multiple_of(i * width, width), width)


def row_sum(x):
    return jnp.sum(x, 0, keepdims=True)


def gelu_parts(x):
    t = 1.0 / (1.0 + (0.3275911 * math.sqrt(0.5)) * jnp.abs(x))
    e = jnp.exp(-0.5 * x * x)
    tail = t * (0.127414796 + t * (-0.142248368 + t * (0.7107068705 + t * (-0.7265760135 + t * 0.5307027145)))) * e
    phi = jnp.where(x >= 0, 1.0 - tail, tail)
    return x * phi, phi + x * (e * (1.0 / math.sqrt(2.0 * math.pi)))


def normed(x):
    centred = x - jnp.mean(x, -1, keepdims=True)
    scale = lax.rsqrt(jnp.mean(centred * centred, -1, keepdims=True) + EPSILON)
    return centred * scale, scale


def norm_back(grad, n, scale, gain):
    gg = gain * grad
    return (gg - jnp.mean(gg, -1, keepdims=True) - n * jnp.mean(gg * n, -1, keepdims=True)) * scale


def kernel(sizes, *refs):
    groups, depth, rs, seq = sizes
    (emb, token_grads, wq_in, wo_in, wu_in, wd_in, lens, scores, bias, gains, head_w,
     out_sec, out_gin, out_q, out_o, out_u, out_d, out_small,
     big, s1, xr, zr, fin, peers,
     hbuf, qkv, probs, mixed, n1, r1, first_low, act, gp, n2, r2, outb, gbuf, high, dd, da, dm, dqkv,
     small, sm_sib, sm_grp, sm_dp, sm_sec,
     local_sem, io_sem, g_zr, g_xr, g_sr, g_send, y_send, y_recv,
     r_send, r_sib, r_x, r_z, r_fin, r_peer, sm_send, sm_recv) = refs
    pairs = 2
    sec = lax.axis_index("section")
    g = lax.axis_index("grp")
    d = lax.axis_index("dp")
    z, c = d // 2, d % 2
    par = g % 2
    first_section = sec == 0

    def dev(sec_=None, g_=None, z_=None, c_=None):
        return (
            sec if sec_ is None else sec_,
            g if g_ is None else g_,
            (z if z_ is None else z_) * 2 + (c if c_ is None else c_),
        )

    sibling = dev(c_=1 - c)
    across = dev(g_=g + 1 - 2 * par)
    other = dev(sec_=1 - sec)

    def rcopy(src, dst, send, recv, to):
        return pltpu.make_async_remote_copy(
            src_ref=src, dst_ref=dst, send_sem=send, recv_sem=recv, device_id=to, device_id_type=MESH
        )

    def shard_row(m, owner, down=DOWN):
        row = jnp.where(m < 8, m * D + owner * rs, down + owner * (4 * rs) + (m - 8) * rs)
        return pl.multiple_of(row, 16)

    barrier = pltpu.get_barrier_semaphore()
    greeted = 0
    for to in [sibling, other]:
        pl.semaphore_signal(barrier, inc=1, device_id=to, device_id_type=MESH)
        greeted += 1
    for k in range(1, groups):
        pl.semaphore_signal(barrier, inc=1, device_id=dev(g_=(g + k) % groups), device_id_type=MESH)
        greeted += 1
    for k in range(1, depth):
        pl.semaphore_signal(barrier, inc=1, device_id=dev(z_=(z + k) % depth), device_id_type=MESH)
        greeted += 1

    own = []
    for k in range(3):
        own.append((wq_in.at[:, pl.ds(k * D, D)], k))
    own.append((wo_in, 3))
    for k in range(4):
        own.append((wu_in.at[:, pl.ds(k * D, D)], 4 + k))
    for src, k in own:
        pltpu.make_async_copy(src, big.at[pl.ds(pl.multiple_of(k * D + d * rs, 16), rs), :], local_sem.at[0]).start()
    pltpu.make_async_copy(
        wd_in, big.at[pl.ds(pl.multiple_of(DOWN + d * 4 * rs, 16), 4 * rs), :], local_sem.at[0]
    ).start()

    @pl.when(first_section)
    def _():
        pltpu.make_async_copy(emb, hbuf, local_sem.at[1]).start()

    @pl.when(~first_section)
    def _():
        pltpu.make_async_copy(token_grads, gbuf, local_sem.at[1]).start()

    small[...] = jnp.zeros_like(small)
    pl.semaphore_wait(barrier, greeted)
    pltpu.make_async_copy(
        big.at[pl.ds(0, CHUNKS * rs), :], big.at[pl.ds(0, CHUNKS * rs), :], local_sem.at[0]
    ).wait()

    def region(m, zz, half=None, cc=c):
        cols = slice(None) if half is None else span(half, HALF)
        return big.at[pl.ds(shard_row(m, 2 * zz + cc), rs), cols]

    def along(m, zz, to):
        part = region(m, zz, par)
        return rcopy(part, part, g_send.at[0], g_zr.at[m, zz], dev(z_=to))

    def over(m, zz, half):
        part = region(m, zz, half)
        return rcopy(part, part, g_send.at[1], g_xr.at[m, zz], across)

    def beside(m, zz, half):
        part = region(m, zz, half)
        return rcopy(part, part, g_send.at[2], g_sr.at[m], sibling)

    def bias_row(start, width=D):
        return bias[:, pl.ds(start, width)]

    low = lax.broadcasted_iota(jnp.int32, (1, 128), 1) < HEAD
    key = lax.broadcasted_iota(jnp.int32, (1, seq), 1)

    def pair_rows(p):
        return span(p, seq)

    def block(k):
        return big[pl.ds(k * D, D), :]

    def project(p, k):
        r = pair_rows(p)
        x = dot(hbuf[r, :], block(k))
        if k != 1:
            x = x + bias_row(0 if k == 0 else D)
        qkv[r, pl.ds(k * D, D)] = x.astype(BF)

    def attend(p):
        r = pair_rows(p)
        ok = key < lens[p]
        for j in range(HEADS // 2):
            q2 = qkv[r, pl.ds(j * 128, 128)]
            k2 = qkv[r, pl.ds((j + 6) * 128, 128)]
            v2 = qkv[r, pl.ds((j + 12) * 128, 128)]
            none = jnp.zeros_like(q2)
            both = jnp.concatenate([jnp.where(low, q2, none), jnp.where(low, none, q2)], 0)
            sc = jnp.where(ok, dot_t(both, k2) * SCALE, -1e30)
            e = jnp.exp(sc - jnp.max(sc, -1, keepdims=True))
            pr = (e * (1.0 / jnp.sum(e, -1, keepdims=True))).astype(BF)
            probs[p * HEADS + 2 * j] = pr[:seq]
            probs[p * HEADS + 2 * j + 1] = pr[seq:]
            o = dot(pr, v2)
            mixed[r, pl.ds(j * 128, 128)] = jnp.where(low, o[:seq], o[seq:]).astype(BF)

    def join(p):
        r = pair_rows(p)
        n, scale = normed(hbuf[r, :].astype(F32) + dot(mixed[r, :], block(3)) + bias_row(2 * D))
        n1[r, :] = n.astype(BF)
        r1[r, :] = scale
        y = n * gains[0:1, :] + bias_row(4 * D + FF)
        high[r, :] = y
        first_low[r, :] = y.astype(BF)

    def widen(p, k):
        r = pair_rows(p)
        for t in range(3):
            w = big[pl.ds((4 + k) * D, D), pl.ds(t * 256, 256)]
            col = k * D + t * 256
            a, dg = gelu_parts(dot(first_low[r, :], w) + bias_row(3 * D + col, 256))
            act[r, pl.ds(col, 256)] = a.astype(BF)
            gp[r, pl.ds(col, 256)] = dg.astype(BF)

    def narrow(p):
        r = pair_rows(p)
        n, scale = normed(high[r, :] + dot(act[r, :], big[pl.ds(DOWN, FF), :]) + bias_row(3 * D + FF))
        n2[r, :] = n.astype(BF)
        r2[r, :] = scale
        y = n * gains[1:2, :] + bias_row(5 * D + FF)
        outb[r, :] = y.astype(BF)

        @pl.when(~first_section)
        def _():
            small[pl.ds(HEAD_ROW, 1), :] += scores[p] * y[0:1]

    def state_copy(p):
        r = pair_rows(p)
        return rcopy(outb.at[r, :], hbuf.at[r, :], y_send.at[0], y_recv.at[p], other)

    def chunk_ready(m):
        whole = big.at[pl.ds(0, depth * rs), :]
        rcopy(whole, whole, g_send.at[2], g_sr.at[m], sibling).wait_recv()

    def own_step(n):
        @pl.when(z > 0)
        def _():
            along(n, z, z - 1).start()

        @pl.when(z < depth - 1)
        def _():
            along(n, z, z + 1).start()

        beside(n, z, None).start()

    def early(step, pieces):
        def run(n):
            @pl.when(first_section & (n == depth + 1 + step))
            def _():
                pieces()

        return run

    def both_pairs(piece):
        @pl.loop(0, pairs)
        def _(p):
            piece(p)

    def early_project(k):
        if k == 0:
            pltpu.make_async_copy(emb, hbuf, local_sem.at[1]).wait()
        chunk_ready(k)
        both_pairs(lambda p: project(p, k))

    def early_join():
        chunk_ready(3)
        both_pairs(join)

    def early_widen(k):
        chunk_ready(4 + k)
        both_pairs(lambda p: widen(p, k))

    plan = [early(k, functools.partial(early_project, k)) for k in range(3)]
    plan.append(early(3, lambda: attend(0)))
    plan.append(early(4, lambda: attend(1)))
    plan.append(early(5, early_join))
    plan += [early(5 + k, functools.partial(early_widen, k)) for k in range(4)]

    @pl.loop(0, CHUNKS + depth)
    def _(n):
        @pl.when(n < CHUNKS)
        def _():
            own_step(n)

        for t in range(1, depth):
            m = n - t
            here = (m >= 0) & (m < CHUNKS)
            for sign in (1, -1):
                zz = z + sign * t

                @pl.when(here & (zz >= 0) & (zz < depth))
                def _(m=m, zz=zz, sign=sign):
                    along(m, zz, z).wait_recv()

                    @pl.when((z - sign >= 0) & (z - sign < depth))
                    def _():
                        along(m, zz, z - sign).start()

                    over(m, zz, par).start()
                    beside(m, zz, par).start()

        for t in range(1, depth):
            m = n - t - 1
            here = (m >= 0) & (m < CHUNKS)
            for sign in (1, -1):
                zz = z + sign * t

                @pl.when(here & (zz >= 0) & (zz < depth))
                def _(m=m, zz=zz):
                    over(m, zz, 1 - par).wait_recv()
                    beside(m, zz, 1 - par).start()

        for run in plan:
            run(n)

    @pl.loop(jnp.where(first_section, 8, 0), CHUNKS)
    def _(m):
        chunk_ready(m)

    @pl.when(first_section)
    def _():
        @pl.loop(0, pairs)
        def _(p):
            narrow(p)
            state_copy(p).start()

    @pl.when(~first_section)
    def _():
        pltpu.make_async_copy(token_grads, gbuf, local_sem.at[1]).wait()

        @pl.loop(0, pairs)
        def _(p):
            state_copy(p).wait_recv()
            for k in range(3):
                project(p, k)
            attend(p)
            join(p)
            for k in range(4):
                widen(p, k)
            narrow(p)

    pltpu.make_async_copy(outb, out_sec, io_sem.at[0]).start()

    for k in range(depth):
        count = (depth - k if k > 0 else 0) + (k + 1 if k < depth - 1 else 0)

        @pl.when(z == k)
        def _(count=count):
            sent = big.at[pl.ds(0, CHUNKS * count * rs), pl.ds(0, HALF)]
            rcopy(sent, sent, g_send.at[0], g_zr.at[0, 0], across).wait_send()

    sent = big.at[pl.ds(0, CHUNKS * (depth - 1) * rs), pl.ds(0, HALF)]
    rcopy(sent, sent, g_send.at[1], g_xr.at[0, 0], across).wait_send()
    sent = big.at[pl.ds(0, CHUNKS * depth * rs), :]
    rcopy(sent, sent, g_send.at[2], g_sr.at[0], sibling).wait_send()

    def add_small(row, x):
        small[pl.ds(row, 1), :] += row_sum(x)

    def outer_norm(p):
        r = pair_rows(p)
        length = jnp.where(first_section, seq, lens[p])
        score = jnp.where(first_section, 0.0, scores[p])
        place = lax.broadcasted_iota(jnp.int32, (seq, 1), 0)
        grad = jnp.where(place < length, gbuf[r, :].astype(F32), 0.0)
        grad = grad + jnp.where(place == 0, score * head_w[...].reshape(1, D), 0.0)
        n = n2[r, :].astype(F32)
        x = norm_back(grad, n, r2[r, :], gains[1:2, :])
        xl = x.astype(BF)
        high[r, :] = x
        dd[r, :] = xl
        add_small(BD, xl.astype(F32))
        add_small(BETA2, grad)
        add_small(GAIN2, grad * n)

    def act_back(p):
        r = pair_rows(p)
        for k in range(4):
            c4 = pl.ds(k * D, D)
            x = (dot_t(dd[r, :], big[pl.ds(DOWN + k * D, D), :]) * gp[r, c4].astype(F32)).astype(BF)
            gp[r, c4] = x
            add_small(BU + k, x.astype(F32))

    def inner_norm(p):
        r = pair_rows(p)
        grad = high[r, :]
        for k in range(4):
            grad = grad + dot_t(gp[r, pl.ds(k * D, D)], block(4 + k))
        n = n1[r, :].astype(F32)
        x = norm_back(grad, n, r1[r, :], gains[0:1, :])
        xl = x.astype(BF)
        high[r, :] = x
        da[r, :] = xl
        add_small(BO, xl.astype(F32))
        add_small(BETA1, grad)
        add_small(GAIN1, grad * n)
        dm[r, :] = dot_t(xl, block(3)).astype(BF)

    def attend_back(p):
        r = pair_rows(p)
        for j in range(HEADS // 2):
            q2 = qkv[r, pl.ds(j * 128, 128)]
            k2 = qkv[r, pl.ds((j + 6) * 128, 128)]
            v2 = qkv[r, pl.ds((j + 12) * 128, 128)]
            d2 = dm[r, pl.ds(j * 128, 128)]
            none = jnp.zeros_like(d2)
            both = jnp.concatenate([jnp.where(low, d2, none), jnp.where(low, none, d2)], 0)
            pr = jnp.concatenate([probs[p * HEADS + 2 * j], probs[p * HEADS + 2 * j + 1]], 0)
            pf = pr.astype(F32)
            t = pf * dot_t(both, v2)
            ds = (t - pf * jnp.sum(t, -1, keepdims=True)).astype(BF)
            dq = dot(ds, k2)
            dq = (jnp.where(low, dq[:seq], dq[seq:]) * SCALE).astype(BF)
            qt, dt = q2.T, d2.T
            dk = jnp.concatenate([dot(qt[:HEAD], ds[:seq]), dot(qt[HEAD:], ds[seq:])], 0)
            dv = jnp.concatenate([dot(dt[:HEAD], pr[:seq]), dot(dt[HEAD:], pr[seq:])], 0)
            dk = (dk * SCALE).astype(BF).T
            dv = dv.astype(BF).T
            dqkv[r, pl.ds(j * 128, 128)] = dq
            dqkv[r, pl.ds((j + 6) * 128, 128)] = dk
            dqkv[r, pl.ds((j + 12) * 128, 128)] = dv
            small[pl.ds(BQ, 1), pl.ds(j * 128, 128)] += row_sum(dq.astype(F32))
            small[pl.ds(BV, 1), pl.ds(j * 128, 128)] += row_sum(dv.astype(F32))

    def hidden_back(p):
        r = pair_rows(p)
        grad = high[r, :]
        for k in range(3):
            grad = grad + dot_t(dqkv[r, pl.ds(k * D, D)], block(k))
        high[r, :] = grad
        outb[r, :] = grad.astype(BF)

    def grad_copy(p):
        r = pair_rows(p)
        return rcopy(outb.at[r, :], gbuf.at[r, :], y_send.at[1], y_recv.at[2 + p], other)

    def weight_grad(left, lcol, right, rcol, row):
        a = left[:, pl.ds(pl.multiple_of(lcol, 256), D)]
        b = right[:, pl.ds(pl.multiple_of(rcol, 256), D)]
        big[pl.ds(pl.multiple_of(row, 256), D), :] = dot_c(a, b).astype(BF)

    def ordered(i):
        return jnp.where(i < 4, i + 8, jnp.where(i < 8, i, jnp.where(i == 8, 3, i - 9)))

    def sib_copy(m, zz):
        return rcopy(
            big.at[pl.ds(shard_row(m, 2 * zz + 1 - c, DOWN_GRAD), rs), :],
            s1.at[m, zz], r_send.at[0], r_sib.at[m], sibling,
        )

    def sib_send(m):
        @pl.loop(0, depth)
        def _(zz):
            sib_copy(m, zz).start()

    def make_down():
        @pl.loop(0, 4)
        def _(k):
            weight_grad(act, k * D, dd, 0, DOWN_GRAD + k * D)

        @pl.loop(8, 12)
        def _(m):
            sib_send(m)

    def make_up():
        @pl.loop(0, 4)
        def _(k):
            weight_grad(first_low, 0, gp, k * D, (4 + k) * D)
            sib_send(4 + k)

    def make_attn():
        weight_grad(mixed, 0, da, 0, 3 * D)
        sib_send(3)

    def make_qkv():
        @pl.loop(0, 3)
        def _(k):
            weight_grad(hbuf, 0, dqkv, k * D, k * D)
            sib_send(k)

    def x_copy(m):
        return rcopy(
            s1.at[m, :, :, span(1 - par, HALF)], xr.at[m], r_send.at[1], r_x.at[m], across
        )

    def z_copy(m, to):
        return rcopy(xr.at[m, to], zr.at[m, z], r_send.at[2], r_z.at[m, z], dev(z_=to))

    def fin_copy(m):
        return rcopy(fin.at[m, par], fin.at[m, par], r_send.at[3], r_fin.at[m], across)

    def pair_sums(m):
        rcopy(s1.at[m], s1.at[m], r_send.at[0], r_sib.at[m], sibling).wait_recv()

        @pl.loop(0, depth)
        def _(zz):
            mine = big[pl.ds(shard_row(m, 2 * zz + c, DOWN_GRAD), rs), :]
            s1[m, zz] = (mine.astype(F32) + s1[m, zz].astype(F32)).astype(BF)

        x_copy(m).start()

    def across_sums(m):
        x_copy(m).wait_recv()

        @pl.loop(0, depth)
        def _(zz):
            mine = s1[m, zz, :, span(par, HALF)]
            xr[m, zz] = (mine.astype(F32) + xr[m, zz].astype(F32)).astype(BF)

        for k in range(1, depth):
            z_copy(m, (z + k) % depth).start()

    def line_sums(m):
        total = xr[m, z].astype(F32)
        for k in range(1, depth):
            zz = (z + k) % depth
            rcopy(xr.at[m, z], zr.at[m, zz], r_send.at[2], r_z.at[m, zz], across).wait_recv()
            total = total + zr[m, zz].astype(F32)
        if groups > 2:
            teams = groups // 2
            team = g // 2
            peers[m, team] = total.astype(BF)
            for k in range(1, teams):
                to = dev(g_=((team + k) % teams) * 2 + par)
                rcopy(peers.at[m, team], peers.at[m, team], r_send.at[4], r_peer.at[m, team], to).start()
            for k in range(1, teams):
                tt = (team + k) % teams
                rcopy(peers.at[m, tt], peers.at[m, tt], r_send.at[4], r_peer.at[m, tt], across).wait_recv()
            total = peers[m, 0].astype(F32)
            for k in range(1, teams):
                total = total + peers[m, k].astype(F32)
        fin[m, par] = total.astype(BF)
        fin_copy(m).start()

    def finish(m):
        rcopy(fin.at[m, 1 - par], fin.at[m, 1 - par], r_send.at[3], r_fin.at[m], across).wait_recv()
        for h in range(2):

            def put(to, row, col, h=h):
                rows = pl.ds(pl.multiple_of(row, 16), rs)
                cols = pl.ds(pl.multiple_of(col + h * HALF, 128), HALF)
                pltpu.make_async_copy(fin.at[m, h], to.at[rows, cols], io_sem.at[2]).start()

            @pl.when(m >= 8)
            def _(put=put):
                put(out_d, (m - 8) * rs, 0)

            @pl.when((m >= 4) & (m < 8))
            def _(put=put):
                put(out_u, 0, (m - 4) * D)

            @pl.when(m == 3)
            def _(put=put):
                put(out_o, 0, 0)

            @pl.when(m < 3)
            def _(put=put):
                put(out_q, 0, m * D)

    stages = (pair_sums, across_sums, line_sums, finish)

    def sum_step(i):
        for lag, stage in enumerate(stages):

            @pl.when((i >= lag) & (i < CHUNKS + lag))
            def _(lag=lag, stage=stage):
                stage(ordered(i - lag))

    pltpu.make_async_copy(outb, out_sec, io_sem.at[0]).wait()

    @pl.when(first_section)
    def _():
        rcopy(outb, outb, y_send.at[0], y_recv.at[0], other).wait_send()

    @pl.loop(0, pairs)
    def _(p):
        start_sums = first_section & (p == pairs - 1)

        @pl.when(first_section)
        def _():
            grad_copy(p).wait_recv()

        outer_norm(p)
        pl.when(start_sums)(make_down)
        act_back(p)

        @pl.when(start_sums)
        def _():
            sum_step(0)

        inner_norm(p)

        @pl.when(start_sums)
        def _():
            make_up()
            sum_step(1)

        attend_back(p)

        @pl.when(start_sums)
        def _():
            sum_step(2)

        hidden_back(p)

        @pl.when(~first_section)
        def _():
            grad_copy(p).start()

    pltpu.make_async_copy(high, out_gin, io_sem.at[1]).start()

    @pl.when(~first_section)
    def _():
        make_down()
        sum_step(0)
        make_up()
        sum_step(1)
        sum_step(2)

    make_attn()
    make_qkv()

    def sm_copy(src, dst, recv, to):
        return rcopy(src, dst, sm_send.at[0], recv, to)

    def small_sib():
        sm_copy(small, sm_sib, sm_recv.at[0], sibling).start()

    def small_grp():
        sm_copy(small, sm_sib, sm_recv.at[0], sibling).wait_recv()
        sm_grp[g] = small[...] + sm_sib[...]
        for k in range(1, groups):
            sm_copy(sm_grp.at[g], sm_grp.at[g], sm_recv.at[1 + g], dev(g_=(g + k) % groups)).start()

    def small_dp():
        for k in range(1, groups):
            gg = (g + k) % groups
            sm_copy(sm_grp.at[gg], sm_grp.at[gg], sm_recv.at[1 + gg], across).wait_recv()
        total = sm_grp[0]
        for k in range(1, groups):
            total = total + sm_grp[k]
        sm_dp[z] = total
        for k in range(1, depth):
            sm_copy(sm_dp.at[z], sm_dp.at[z], sm_recv.at[1 + groups + z], dev(z_=(z + k) % depth)).start()

    def head_copy():
        return rcopy(out_small, sm_sec, sm_send.at[1], sm_recv.at[1 + groups + depth], other)

    def small_sec():
        for k in range(1, depth):
            zz = (z + k) % depth
            sm_copy(sm_dp.at[zz], sm_dp.at[zz], sm_recv.at[1 + groups + zz], across).wait_recv()
        total = sm_dp[0]
        for k in range(1, depth):
            total = total + sm_dp[k]
        out_small[...] = total

        @pl.when(~first_section)
        def _():
            head_copy().start()

    def small_head():
        @pl.when(first_section)
        def _():
            head_copy().wait_recv()
            out_small[pl.ds(HEAD_ROW, 1), :] = sm_sec[pl.ds(HEAD_ROW, 1), :]

        @pl.when(~first_section)
        def _():
            head_copy().wait_send()

    @pl.loop(3, CHUNKS + len(stages) - 1)
    def _(i):
        for at, part in ((3, small_sib), (5, small_grp), (7, small_dp), (9, small_sec), (11, small_head)):
            pl.when(i == at)(part)
        sum_step(i)

    count = 1 + (groups - 1) + (depth - 1)
    sent = high.at[pl.ds(0, count * SMALL), :]
    rcopy(sent, sent, sm_send.at[0], sm_recv.at[0], other).wait_send()

    @pl.when(~first_section)
    def _():
        rcopy(outb, outb, y_send.at[1], y_recv.at[0], other).wait_send()

    pltpu.make_async_copy(high, out_gin, io_sem.at[1]).wait()
    pltpu.make_async_copy(fin, fin, io_sem.at[2]).wait()
    rcopy(s1, s1, r_send.at[0], r_sib.at[0], sibling).wait_send()
    rcopy(xr, xr, r_send.at[1], r_x.at[0], across).wait_send()
    part = zr.at[:, pl.ds(0, depth - 1)]
    rcopy(part, part, r_send.at[2], r_z.at[0, 0], across).wait_send()
    part = fin.at[:, 0]
    rcopy(part, part, r_send.at[3], r_fin.at[0], across).wait_send()
    if groups > 2:
        part = peers.at[:, pl.ds(0, groups // 2 - 1)]
        rcopy(part, part, r_send.at[4], r_peer.at[0, 0], across).wait_send()


def on_device(groups, depth, embedded, lengths, token_grads, score_grads, w_qkv, w_attn_out, w_up, w_down, biases, gains, head_weight):
    micro, _, seq, _ = embedded.shape
    tokens = micro * seq
    rs = w_qkv.shape[1]
    vmem = pl.BlockSpec(memory_space=pltpu.VMEM)
    smem = pl.BlockSpec(memory_space=pltpu.SMEM)
    hbm = pl.BlockSpec(memory_space=pl.ANY)
    teams = max(groups // 2, 1)
    out_shape = (
        jax.ShapeDtypeStruct((tokens, D), BF),
        jax.ShapeDtypeStruct((tokens, D), F32),
        jax.ShapeDtypeStruct((rs, 3 * D), BF),
        jax.ShapeDtypeStruct((rs, D), BF),
        jax.ShapeDtypeStruct((rs, FF), BF),
        jax.ShapeDtypeStruct((4 * rs, D), BF),
        jax.ShapeDtypeStruct((SMALL, D), F32),
    )
    scratch = [
        pltpu.VMEM((CHUNKS * D + FF, D), BF),
        pltpu.VMEM((CHUNKS, depth, rs, D), BF),
        pltpu.VMEM((CHUNKS, depth, rs, HALF), BF),
        pltpu.VMEM((CHUNKS, depth, rs, HALF), BF),
        pltpu.VMEM((CHUNKS, 2, rs, HALF), BF),
        pltpu.VMEM((CHUNKS, teams, rs, HALF) if groups > 2 else (1, 1, 16, 128), BF),
        pltpu.VMEM((tokens, D), BF),
        pltpu.VMEM((tokens, 3 * D), BF),
        pltpu.VMEM((micro * HEADS, seq, seq), BF),
        pltpu.VMEM((tokens, D), BF),
        pltpu.VMEM((tokens, D), BF),
        pltpu.VMEM((tokens, 1), F32),
        pltpu.VMEM((tokens, D), BF),
        pltpu.VMEM((tokens, FF), BF),
        pltpu.VMEM((tokens, FF), BF),
        pltpu.VMEM((tokens, D), BF),
        pltpu.VMEM((tokens, 1), F32),
        pltpu.VMEM((tokens, D), BF),
        pltpu.VMEM((tokens, D), BF),
        pltpu.VMEM((tokens, D), F32),
        pltpu.VMEM((tokens, D), BF),
        pltpu.VMEM((tokens, D), BF),
        pltpu.VMEM((tokens, D), BF),
        pltpu.VMEM((tokens, 3 * D), BF),
        pltpu.VMEM((SMALL, D), F32),
        pltpu.VMEM((SMALL, D), F32),
        pltpu.VMEM((groups, SMALL, D), F32),
        pltpu.VMEM((depth, SMALL, D), F32),
        pltpu.VMEM((SMALL, D), F32),
        pltpu.SemaphoreType.DMA((2,)),
        pltpu.SemaphoreType.DMA((3,)),
        pltpu.SemaphoreType.DMA((CHUNKS, depth)),
        pltpu.SemaphoreType.DMA((CHUNKS, depth)),
        pltpu.SemaphoreType.DMA((CHUNKS,)),
        pltpu.SemaphoreType.DMA((3,)),
        pltpu.SemaphoreType.DMA((2,)),
        pltpu.SemaphoreType.DMA((4,)),
        pltpu.SemaphoreType.DMA((5,)),
        pltpu.SemaphoreType.DMA((CHUNKS,)),
        pltpu.SemaphoreType.DMA((CHUNKS,)),
        pltpu.SemaphoreType.DMA((CHUNKS, depth)),
        pltpu.SemaphoreType.DMA((CHUNKS,)),
        pltpu.SemaphoreType.DMA((CHUNKS, teams)),
        pltpu.SemaphoreType.DMA((2,)),
        pltpu.SemaphoreType.DMA((2 + groups + depth,)),
    ]
    state, grad_in, *grads, small = pl.pallas_call(
        functools.partial(kernel, (groups, depth, rs, seq)),
        out_shape=out_shape,
        in_specs=[hbm] * 6 + [smem] * 2 + [vmem] * 3,
        out_specs=(hbm,) * 6 + (vmem,),
        scratch_shapes=scratch,
        compiler_params=pltpu.CompilerParams(
            collective_id=0, has_side_effects=True, vmem_limit_bytes=63 * 1024 * 1024
        ),
    )(
        embedded.reshape(tokens, D),
        token_grads.reshape(tokens, D),
        w_qkv[0],
        w_attn_out[0],
        w_up[0],
        w_down[0],
        lengths.reshape(micro),
        score_grads.reshape(micro),
        biases,
        gains[0],
        head_weight,
    )
    results = pl.pallas_call(
        hand_out,
        out_shape=[jax.ShapeDtypeStruct(x.shape, x.dtype) for x in (state, grad_in)]
        + [jax.ShapeDtypeStruct(x.shape, F32) for x in grads]
        + [jax.ShapeDtypeStruct(x, F32) for x in ((1, 10 * D), (2, D), (D,))],
        in_specs=[vmem] * 7,
        out_specs=[vmem] * 9,
    )(state, grad_in, *grads, small)
    state, grad_in, g_qkv, g_attn, g_up, g_down, g_bias, g_gain, g_head = results
    return (
        state.reshape(1, micro, 1, seq, D),
        grad_in.reshape(1, micro, 1, seq, D),
        g_qkv[None],
        g_attn[None],
        g_up[None],
        g_down[None],
        g_bias,
        g_gain[None],
        g_head,
    )


def hand_out(state, grad_in, gq, go, gu, gd, small, o_state, o_gin, o_q, o_o, o_u, o_d, o_bias, o_gain, o_head):
    for src, dst in ((state, o_state), (grad_in, o_gin), (gq, o_q), (go, o_o), (gu, o_u), (gd, o_d)):
        dst[...] = src[...].astype(dst.dtype)
    for k in range(10):
        o_bias[:, pl.ds(k * D, D)] = small[pl.ds(k, 1), :]
    o_gain[...] = small[pl.ds(GAIN1, 2), :]
    o_head[...] = small[HEAD_ROW, :]


def solution(mesh):
    return jax.shard_map(
        functools.partial(on_device, mesh.shape["grp"], mesh.shape["dp"] // 2),
        mesh=mesh,
        in_specs=(
            P(None, ("grp", "dp"), None, None),
            P(None, ("grp", "dp")),
            P(None, ("grp", "dp"), None, None),
            P(None, ("grp", "dp")),
            P("section", "dp", None),
            P("section", "dp", None),
            P("section", "dp", None),
            P("section", "dp", None),
            P("section", None),
            P("section", None, None),
            P(),
        ),
        out_specs=(
            P("section", None, ("grp", "dp"), None, None),
            P("section", None, ("grp", "dp"), None, None),
            P("section", "dp", None),
            P("section", "dp", None),
            P("section", "dp", None),
            P("section", "dp", None),
            P("section", None),
            P("section", None, None),
            P(),
        ),
        check_vma=False,
    )
```

time: 960 us -> 250 us (0.26); the launches traced: 947 us -> 250 us
  waiting for transfers between devices: 598 us -> 0 us
  Pallas kernels: 0 us -> 249 us
  local copies, waits for them, and re-layouts: 122 us -> 0 us
  matrix products: 108 us -> 0 us
  other arithmetic: 81.4 us -> 0 us
  between operations: 16.9 us -> 0.65 us
  loops' own time: 11.7 us -> 0 us
  starting transfers between devices: 9.71 us -> 0 us
    pallas_call x0 -> x2, Pallas kernels: none -> 249 us  [the longest x1 244 us: on_device(): pl.pallas_call(functools.partial(kernel, (groups, depth, rs, seq)), out_s...]
    psum x2 -> x0, waiting for transfers between devices: 179 us -> none  [the longest x1 121 us: on_device(): lax.psum((bias_place, gain_place, head_total), ('section', 'grp', 'dp'))]
    all_gather x4 -> x0, waiting for transfers between devices: 169 us -> none  [the longest x1 52.3 us: on_device(): lax.all_gather(w_up[0], 'dp', axis=0, tiled=True)]
    reduce_scatter x4 -> x0, waiting for transfers between devices: 148 us -> none  [the longest x1 55.9 us: on_device(): lax.psum_scatter(terms[3].astype(jnp.bfloat16), 'dp', scatter_dimension=0...]
    dot_general x34 -> x0, matrix products: 108 us -> none  [the longest x8 39.5 us: times_trans(): lax.dot_general(left_rows, right_rows, (((1,), (1,)), ((), ())), preferre...]
    ppermute x4 -> x0, waiting for transfers between devices: 98.8 us -> none  [passed_along(): return lax.ppermute(x, axis, pairs)]
    another operation x36 -> x0, local copies, waits for them, and re-layouts: 39.2 us -> none  [the longest x18 24.3 us: on_device(): jnp.stack([tick_rec[member] for tick_rec in record_list])]
    unnamed x99 -> x0, local copies, waits for them, and re-layouts: 33.1 us -> none
  transfers between devices with their start and end apart: 14 -> 0, of which waited for: 13 -> 0; matrix products, arithmetic and copies ran while one was open for 7% -> 0% of each run, Pallas kernels for 0% -> 0%
where the time goes in v1:
time: 250 us
  Pallas kernels  249 us (100%)
    pallas_call x1, Pallas kernels, on_device(): pl.pallas_call(functools.partial(kernel, (groups, depth, rs, seq)), out_s...  244 us

profile of v1, /device:TPU:0, one launch (start us, length us, event | category | flops | bytes accessed | tf_op | source)
XLA Modules:
  0.0 249.8 jit_solution(16283691652065432171)
XLA Ops:
  0.6 244.3 %shard_map.178 = (bf16[512,768]{1,0:T(8,128)(2,1)}, f32[512,768]{1,0:T(8,128)}, bf16[96,2304]{1,0:T(8,128)(2,1)}, bf16[96,768]{1,0:T(8,128)(2,1)}, bf16[96,3072]...) custom-call(bf16[512,768]{1,0:T(8,128)(2,1)} %bitcast.20, bf16[512,768]{1,0:T(8,128)(2,1)} %bitcast.21, ...), custom_call_target="tpu_custom_call" | custom-call | tf_op jit(solution)/shard_map/pallas_call | solution.py:760
  244.9 4.8 %shard_map.179 = (bf16[512,768]{1,0:T(8,128)(2,1)}, f32[512,768]{1,0:T(8,128)}, f32[96,2304]{1,0:T(8,128)}, f32[96,768]{1,0:T(8,128)}, f32[96,3072]{1,0:T(8,128)...) custom-call(bf16[512,768]{1,0:T(8,128)(2,1)} %get-tuple-element.25.state, ...), custom_call_target="tpu_custom_call" | custom-call | tf_op jit(solution)/shard_map/pallas_call | solution.py:782

commit v2 on v1

--- a/solution.py
+++ b/solution.py
@@ -23,6 +23,8 @@
 MESH = pl.DeviceIdType.MESH
 BQ, BV, BO, BU, BD, BETA1, BETA2, GAIN1, GAIN2, HEAD_ROW = 0, 1, 2, 3, 7, 8, 9, 10, 11, 12
 SMALL = 16
+X_FIRST = (8, 4, 5, 6, 3, 0, 1, 2)
+Z_FIRST = (9, 10, 11, 7)
 
 
 def dot(a, b):
@@ -39,6 +41,29 @@
 
 def span(i, width):
     return pl.ds(pl.multiple_of(i * width, width), width)
+
+
+def flip(index, mask):
+    bit = 1
+    while bit <= mask:
+        if mask & bit:
+            index = index + bit - 2 * bit * ((index // bit) % 2)
+        bit *= 2
+    return index
+
+
+def masks(bits):
+    found = [0]
+    for bit in bits:
+        found = found + [mask ^ bit for mask in found]
+    return found
+
+
+def pick(i, values):
+    found = values[-1]
+    for k in range(len(values) - 2, -1, -1):
+        found = jnp.where(i == k, values[k], found)
+    return found
 
 
 def row_sum(x):
@@ -68,11 +93,12 @@
     groups, depth, rs, seq = sizes
     (emb, token_grads, wq_in, wo_in, wu_in, wd_in, lens, scores, bias, gains, head_w,
      out_sec, out_gin, out_q, out_o, out_u, out_d, out_small,
-     big, s1, xr, zr, fin, peers,
+     big, s1, xr, zr, zw, xw, fin, peers,
      hbuf, qkv, probs, mixed, n1, r1, first_low, act, gp, n2, r2, outb, gbuf, high, dd, da, dm, dqkv,
      small, sm_sib, sm_grp, sm_dp, sm_sec,
      local_sem, io_sem, g_zr, g_xr, g_sr, g_send, y_send, y_recv,
-     r_send, r_sib, r_x, r_z, r_fin, r_peer, sm_send, sm_recv) = refs
+     r_send, r_sib, r_x, r_z, r_grp, r_fin, r_peer, sm_send, sm_recv) = refs
+    stages = depth.bit_length() - 1
     pairs = 2
     sec = lax.axis_index("section")
     g = lax.axis_index("grp")
@@ -143,9 +169,12 @@
         cols = slice(None) if half is None else span(half, HALF)
         return big.at[pl.ds(shard_row(m, 2 * zz + cc), rs), cols]
 
-    def along(m, zz, to):
+    far = [depth >> (t + 1) for t in range(stages)]
+    held = [masks(far[:t]) for t in range(stages + 1)]
+
+    def along(m, zz, t):
         part = region(m, zz, par)
-        return rcopy(part, part, g_send.at[0], g_zr.at[m, zz], dev(z_=to))
+        return rcopy(part, part, g_send.at[0], g_zr.at[m, zz], dev(z_=flip(z, far[t])))
 
     def over(m, zz, half):
         part = region(m, zz, half)
@@ -230,19 +259,29 @@
         rcopy(whole, whole, g_send.at[2], g_sr.at[m], sibling).wait_recv()
 
     def own_step(n):
-        @pl.when(z > 0)
-        def _():
-            along(n, z, z - 1).start()
-
-        @pl.when(z < depth - 1)
-        def _():
-            along(n, z, z + 1).start()
-
+        if stages:
+            along(n, z, 0).start()
         beside(n, z, None).start()
+
+    def arrived(m, t):
+        for mask in held[t]:
+            zz = flip(z, far[t] ^ mask)
+            along(m, zz, t).wait_recv()
+            over(m, zz, par).start()
+            beside(m, zz, par).start()
+        if t + 1 < stages:
+            for mask in held[t + 1]:
+                along(m, flip(z, mask), t + 1).start()
+
+    def crossed(m, t):
+        for mask in held[t]:
+            zz = flip(z, far[t] ^ mask)
+            over(m, zz, 1 - par).wait_recv()
+            beside(m, zz, 1 - par).start()
 
     def early(step, pieces):
         def run(n):
-            @pl.when(first_section & (n == depth + 1 + step))
+            @pl.when(first_section & (n == stages + 2 + step))
             def _():
                 pieces()
 
@@ -273,40 +312,15 @@
     plan.append(early(5, early_join))
     plan += [early(5 + k, functools.partial(early_widen, k)) for k in range(4)]
 
-    @pl.loop(0, CHUNKS + depth)
+    @pl.loop(0, CHUNKS + stages + 1)
     def _(n):
-        @pl.when(n < CHUNKS)
-        def _():
-            own_step(n)
-
-        for t in range(1, depth):
-            m = n - t
-            here = (m >= 0) & (m < CHUNKS)
-            for sign in (1, -1):
-                zz = z + sign * t
-
-                @pl.when(here & (zz >= 0) & (zz < depth))
-                def _(m=m, zz=zz, sign=sign):
-                    along(m, zz, z).wait_recv()
-
-                    @pl.when((z - sign >= 0) & (z - sign < depth))
-                    def _():
-                        along(m, zz, z - sign).start()
-
-                    over(m, zz, par).start()
-                    beside(m, zz, par).start()
-
-        for t in range(1, depth):
+        pl.when(n < CHUNKS)(functools.partial(own_step, n))
+        for t in range(stages):
             m = n - t - 1
-            here = (m >= 0) & (m < CHUNKS)
-            for sign in (1, -1):
-                zz = z + sign * t
-
-                @pl.when(here & (zz >= 0) & (zz < depth))
-                def _(m=m, zz=zz):
-                    over(m, zz, 1 - par).wait_recv()
-                    beside(m, zz, 1 - par).start()
-
+            pl.when((m >= 0) & (m < CHUNKS))(functools.partial(arrived, m, t))
+        for t in range(stages):
+            m = n - t - 2
+            pl.when((m >= 0) & (m < CHUNKS))(functools.partial(crossed, m, t))
         for run in plan:
             run(n)
 
@@ -338,14 +352,8 @@
 
     pltpu.make_async_copy(outb, out_sec, io_sem.at[0]).start()
 
-    for k in range(depth):
-        count = (depth - k if k > 0 else 0) + (k + 1 if k < depth - 1 else 0)
-
-        @pl.when(z == k)
-        def _(count=count):
-            sent = big.at[pl.ds(0, CHUNKS * count * rs), pl.ds(0, HALF)]
-            rcopy(sent, sent, g_send.at[0], g_zr.at[0, 0], across).wait_send()
-
+    sent = big.at[pl.ds(0, CHUNKS * (depth - 1) * rs), pl.ds(0, HALF)]
+    rcopy(sent, sent, g_send.at[0], g_zr.at[0, 0], across).wait_send()
     sent = big.at[pl.ds(0, CHUNKS * (depth - 1) * rs), pl.ds(0, HALF)]
     rcopy(sent, sent, g_send.at[1], g_xr.at[0, 0], across).wait_send()
     sent = big.at[pl.ds(0, CHUNKS * depth * rs), :]
@@ -436,9 +444,6 @@
         b = right[:, pl.ds(pl.multiple_of(rcol, 256), D)]
         big[pl.ds(pl.multiple_of(row, 256), D), :] = dot_c(a, b).astype(BF)
 
-    def ordered(i):
-        return jnp.where(i < 4, i + 8, jnp.where(i < 8, i, jnp.where(i == 8, 3, i - 9)))
-
     def sib_copy(m, zz):
         return rcopy(
             big.at[pl.ds(shard_row(m, 2 * zz + 1 - c, DOWN_GRAD), rs), :],
@@ -475,17 +480,6 @@
             weight_grad(hbuf, 0, dqkv, k * D, k * D)
             sib_send(k)
 
-    def x_copy(m):
-        return rcopy(
-            s1.at[m, :, :, span(1 - par, HALF)], xr.at[m], r_send.at[1], r_x.at[m], across
-        )
-
-    def z_copy(m, to):
-        return rcopy(xr.at[m, to], zr.at[m, z], r_send.at[2], r_z.at[m, z], dev(z_=to))
-
-    def fin_copy(m):
-        return rcopy(fin.at[m, par], fin.at[m, par], r_send.at[3], r_fin.at[m], across)
-
     def pair_sums(m):
         rcopy(s1.at[m], s1.at[m], r_send.at[0], r_sib.at[m], sibling).wait_recv()
 
@@ -494,43 +488,24 @@
             mine = big[pl.ds(shard_row(m, 2 * zz + c, DOWN_GRAD), rs), :]
             s1[m, zz] = (mine.astype(F32) + s1[m, zz].astype(F32)).astype(BF)
 
-        x_copy(m).start()
-
-    def across_sums(m):
-        x_copy(m).wait_recv()
-
-        @pl.loop(0, depth)
-        def _(zz):
-            mine = s1[m, zz, :, span(par, HALF)]
-            xr[m, zz] = (mine.astype(F32) + xr[m, zz].astype(F32)).astype(BF)
-
-        for k in range(1, depth):
-            z_copy(m, (z + k) % depth).start()
-
-    def line_sums(m):
-        total = xr[m, z].astype(F32)
-        for k in range(1, depth):
-            zz = (z + k) % depth
-            rcopy(xr.at[m, z], zr.at[m, zz], r_send.at[2], r_z.at[m, zz], across).wait_recv()
-            total = total + zr[m, zz].astype(F32)
-        if groups > 2:
-            teams = groups // 2
-            team = g // 2
-            peers[m, team] = total.astype(BF)
-            for k in range(1, teams):
-                to = dev(g_=((team + k) % teams) * 2 + par)
-                rcopy(peers.at[m, team], peers.at[m, team], r_send.at[4], r_peer.at[m, team], to).start()
-            for k in range(1, teams):
-                tt = (team + k) % teams
-                rcopy(peers.at[m, tt], peers.at[m, tt], r_send.at[4], r_peer.at[m, tt], across).wait_recv()
-            total = peers[m, 0].astype(F32)
-            for k in range(1, teams):
-                total = total + peers[m, k].astype(F32)
-        fin[m, par] = total.astype(BF)
-        fin_copy(m).start()
-
-    def finish(m):
-        rcopy(fin.at[m, 1 - par], fin.at[m, 1 - par], r_send.at[3], r_fin.at[m], across).wait_recv()
+    sides = [masks([2 << k for k in range(t, stages - 1)]) for t in range(stages)]
+    slots = [sum(len(side) for side in sides[:t]) for t in range(stages)]
+
+    def line_send(part, landing, m, t, send):
+        for k, mask in enumerate(sides[t]):
+            rcopy(
+                part.at[flip(z, (1 << t) ^ mask)], landing.at[slots[t] + k], send, r_z.at[m, t],
+                dev(z_=flip(z, 1 << t)),
+            ).start()
+
+    def line_add(part, landing, m, t, send):
+        here = landing.at[pl.ds(slots[t], len(sides[t]))]
+        rcopy(here, here, send, r_z.at[m, t], dev(z_=flip(z, 1 << t))).wait_recv()
+        for k, mask in enumerate(sides[t]):
+            zz = flip(z, mask)
+            part[zz] = (part[zz].astype(F32) + landing[slots[t] + k].astype(F32)).astype(BF)
+
+    def put_out(m):
         for h in range(2):
 
             def put(to, row, col, h=h):
@@ -554,14 +529,98 @@
             def _(put=put):
                 put(out_q, 0, m * D)
 
-    stages = (pair_sums, across_sums, line_sums, finish)
+    def x_copy(q, m):
+        return rcopy(
+            s1.at[m, :, :, span(1 - par, HALF)], xr.at[q], r_send.at[1], r_x.at[m], across
+        )
+
+    def fin_copy(m):
+        return rcopy(fin.at[m, par], fin.at[m, par], r_send.at[4], r_fin.at[m], across)
+
+    def x_start(q, m):
+        pair_sums(m)
+        x_copy(q, m).start()
+
+    def x_halves(q, m):
+        x_copy(q, m).wait_recv()
+
+        @pl.loop(0, depth)
+        def _(zz):
+            mine = s1[m, zz, :, span(par, HALF)]
+            xr[q, zz] = (mine.astype(F32) + xr[q, zz].astype(F32)).astype(BF)
+
+        line_send(xr.at[q], zr.at[q], m, 0, r_send.at[2])
+
+    def x_line(t, q, m):
+        line_add(xr.at[q], zr.at[q], m, t, r_send.at[2])
+        if t + 1 < stages:
+            line_send(xr.at[q], zr.at[q], m, t + 1, r_send.at[2])
+            return
+        total = xr[q, z]
+        if groups > 2:
+            teams = groups // 2
+            team = g // 2
+            peers[q, team] = total
+            for k in range(1, teams):
+                to = dev(g_=((team + k) % teams) * 2 + par)
+                rcopy(peers.at[q, team], peers.at[q, team], r_send.at[5], r_peer.at[m, team], to).start()
+            for k in range(1, teams):
+                tt = (team + k) % teams
+                rcopy(peers.at[q, tt], peers.at[q, tt], r_send.at[5], r_peer.at[m, tt], across).wait_recv()
+            total = peers[q, 0].astype(F32)
+            for k in range(1, teams):
+                total = total + peers[q, k].astype(F32)
+            total = total.astype(BF)
+        fin[m, par] = total
+        fin_copy(m).start()
+
+    def x_finish(q, m):
+        rcopy(fin.at[m, 1 - par], fin.at[m, 1 - par], r_send.at[4], r_fin.at[m], across).wait_recv()
+        put_out(m)
+
+    def z_start(q, m):
+        pair_sums(m)
+        line_send(s1.at[m], zw.at[q], m, 0, r_send.at[3])
+
+    def z_line(t, q, m):
+        line_add(s1.at[m], zw.at[q], m, t, r_send.at[3])
+        if t + 1 < stages:
+            line_send(s1.at[m], zw.at[q], m, t + 1, r_send.at[3])
+            return
+        xw[q, g] = s1[m, z]
+        for k in range(1, groups):
+            rcopy(xw.at[q, g], xw.at[q, g], r_send.at[6], r_grp.at[q, g], dev(g_=(g + k) % groups)).start()
+
+    def z_finish(q, m):
+        for k in range(1, groups):
+            gg = (g + k) % groups
+            rcopy(xw.at[q, gg], xw.at[q, gg], r_send.at[6], r_grp.at[q, gg], across).wait_recv()
+        total = xw[q, 0].astype(F32)
+        for k in range(1, groups):
+            total = total + xw[q, k].astype(F32)
+        total = total.astype(BF)
+        fin[m, 0] = total[:, :HALF]
+        fin[m, 1] = total[:, HALF:]
+        put_out(m)
+
+    x_stages = [x_start, x_halves] + [functools.partial(x_line, t) for t in range(stages)] + [x_finish]
+    z_stages = [z_start] + [functools.partial(z_line, t) for t in range(stages)] + [z_finish]
+    steps = max(len(X_FIRST) + len(x_stages), 2 * len(Z_FIRST) - 1 + len(z_stages)) - 1
 
     def sum_step(i):
-        for lag, stage in enumerate(stages):
-
-            @pl.when((i >= lag) & (i < CHUNKS + lag))
-            def _(lag=lag, stage=stage):
-                stage(ordered(i - lag))
+        for lag in range(max(len(x_stages), len(z_stages))):
+            if lag < len(x_stages):
+
+                @pl.when((i >= lag) & (i < len(X_FIRST) + lag))
+                def _(lag=lag):
+                    x_stages[lag](i - lag, pick(i - lag, X_FIRST))
+
+            if lag < len(z_stages):
+
+                @pl.when((i >= lag) & (i < 2 * len(Z_FIRST) + lag) & ((i - lag) % 2 == 0))
+                def _(lag=lag):
+                    q = (i - lag) // 2
+                    z_stages[lag](q, pick(q, Z_FIRST))
 
     pltpu.make_async_copy(outb, out_sec, io_sem.at[0]).wait()
 
@@ -666,9 +725,9 @@
         def _():
             head_copy().wait_send()
 
-    @pl.loop(3, CHUNKS + len(stages) - 1)
+    @pl.loop(3, steps)
     def _(i):
-        for at, part in ((3, small_sib), (5, small_grp), (7, small_dp), (9, small_sec), (11, small_head)):
+        for at, part in ((3, small_sib), (4, small_grp), (5, small_dp), (6, small_sec), (8, small_head)):
             pl.when(i == at)(part)
         sum_step(i)
 
@@ -684,13 +743,16 @@
     pltpu.make_async_copy(fin, fin, io_sem.at[2]).wait()
     rcopy(s1, s1, r_send.at[0], r_sib.at[0], sibling).wait_send()
     rcopy(xr, xr, r_send.at[1], r_x.at[0], across).wait_send()
-    part = zr.at[:, pl.ds(0, depth - 1)]
-    rcopy(part, part, r_send.at[2], r_z.at[0, 0], across).wait_send()
-    part = fin.at[:, 0]
-    rcopy(part, part, r_send.at[3], r_fin.at[0], across).wait_send()
+    if stages:
+        rcopy(zr, zr, r_send.at[2], r_z.at[0, 0], across).wait_send()
+        rcopy(zw, zw, r_send.at[3], r_z.at[0, 0], across).wait_send()
+    part = fin.at[pl.ds(0, len(X_FIRST)), 0]
+    rcopy(part, part, r_send.at[4], r_fin.at[0], across).wait_send()
     if groups > 2:
         part = peers.at[:, pl.ds(0, groups // 2 - 1)]
-        rcopy(part, part, r_send.at[4], r_peer.at[0, 0], across).wait_send()
+        rcopy(part, part, r_send.at[5], r_peer.at[0, 0], across).wait_send()
+    part = xw.at[:, pl.ds(0, groups - 1)]
+    rcopy(part, part, r_send.at[6], r_grp.at[0, 0], across).wait_send()
 
 
 def on_device(groups, depth, embedded, lengths, token_grads, score_grads, w_qkv, w_attn_out, w_up, w_down, biases, gains, head_weight):
@@ -701,6 +763,7 @@
     smem = pl.BlockSpec(memory_space=pltpu.SMEM)
     hbm = pl.BlockSpec(memory_space=pl.ANY)
     teams = max(groups // 2, 1)
+    stages = depth.bit_length() - 1
     out_shape = (
         jax.ShapeDtypeStruct((tokens, D), BF),
         jax.ShapeDtypeStruct((tokens, D), F32),
@@ -710,13 +773,16 @@
         jax.ShapeDtypeStruct((4 * rs, D), BF),
         jax.ShapeDtypeStruct((SMALL, D), F32),
     )
+    nx, nz = len(X_FIRST), len(Z_FIRST)
     scratch = [
         pltpu.VMEM((CHUNKS * D + FF, D), BF),
         pltpu.VMEM((CHUNKS, depth, rs, D), BF),
-        pltpu.VMEM((CHUNKS, depth, rs, HALF), BF),
-        pltpu.VMEM((CHUNKS, depth, rs, HALF), BF),
+        pltpu.VMEM((nx, depth, rs, HALF), BF),
+        pltpu.VMEM((nx, max(depth - 1, 1), rs, HALF), BF),
+        pltpu.VMEM((nz, max(depth - 1, 1), rs, D), BF),
+        pltpu.VMEM((nz, groups, rs, D), BF),
         pltpu.VMEM((CHUNKS, 2, rs, HALF), BF),
-        pltpu.VMEM((CHUNKS, teams, rs, HALF) if groups > 2 else (1, 1, 16, 128), BF),
+        pltpu.VMEM((nx, teams, rs, HALF) if groups > 2 else (1, 1, 16, 128), BF),
         pltpu.VMEM((tokens, D), BF),
         pltpu.VMEM((tokens, 3 * D), BF),
         pltpu.VMEM((micro * HEADS, seq, seq), BF),
@@ -748,10 +814,11 @@
         pltpu.SemaphoreType.DMA((3,)),
         pltpu.SemaphoreType.DMA((2,)),
         pltpu.SemaphoreType.DMA((4,)),
-        pltpu.SemaphoreType.DMA((5,)),
+        pltpu.SemaphoreType.DMA((7,)),
         pltpu.SemaphoreType.DMA((CHUNKS,)),
         pltpu.SemaphoreType.DMA((CHUNKS,)),
-        pltpu.SemaphoreType.DMA((CHUNKS, depth)),
+        pltpu.SemaphoreType.DMA((CHUNKS, max(stages, 1))),
+        pltpu.SemaphoreType.DMA((nz, groups)),
         pltpu.SemaphoreType.DMA((CHUNKS,)),
         pltpu.SemaphoreType.DMA((CHUNKS, teams)),
         pltpu.SemaphoreType.DMA((2,)),

time: 250 us -> 238 us (0.952)
  Pallas kernels: 249 us -> 237 us
    pallas_call x1, Pallas kernels: 244 us -> 232 us  [on_device(): pl.pallas_call(functools.partial(kernel, (groups, depth, rs, seq)), out_s...]
where the time goes in v2:
time: 238 us; the launch traced here: 237 us
  Pallas kernels  237 us (100%)
    pallas_call x1, Pallas kernels, on_device(): pl.pallas_call(functools.partial(kernel, (groups, depth, rs, seq)), out_s...  232 us
    pallas_call x1, Pallas kernels, on_device(): pl.pallas_call(hand_out, out_shape=[jax.ShapeDtypeStruct(x.shape, x.dtype...  4.81 us

profile of v2, /device:TPU:0, one launch (start us, length us, event | category | flops | bytes accessed | tf_op | source)
XLA Modules:
  0.0 237.3 jit_solution(7191313057949785402)
XLA Ops:
  0.6 231.9 %shard_map.178 = (bf16[512,768]{1,0:T(8,128)(2,1)}, f32[512,768]{1,0:T(8,128)}, bf16[96,2304]{1,0:T(8,128)(2,1)}, bf16[96,768]{1,0:T(8,128)(2,1)}, bf16[96,3072]...) custom-call(bf16[512,768]{1,0:T(8,128)(2,1)} %bitcast.20, bf16[512,768]{1,0:T(8,128)(2,1)} %bitcast.21, ...), custom_call_target="tpu_custom_call" | custom-call | tf_op jit(solution)/shard_map/pallas_call | solution.py:827
  232.5 4.8 %shard_map.179 = (bf16[512,768]{1,0:T(8,128)(2,1)}, f32[512,768]{1,0:T(8,128)}, f32[96,2304]{1,0:T(8,128)}, f32[96,768]{1,0:T(8,128)}, f32[96,3072]{1,0:T(8,128)...) custom-call(bf16[512,768]{1,0:T(8,128)(2,1)} %get-tuple-element.25.state, ...), custom_call_target="tpu_custom_call" | custom-call | tf_op jit(solution)/shard_map/pallas_call | solution.py:849

commit v3 on v2

--- a/solution.py
+++ b/solution.py
@@ -23,8 +23,24 @@
 MESH = pl.DeviceIdType.MESH
 BQ, BV, BO, BU, BD, BETA1, BETA2, GAIN1, GAIN2, HEAD_ROW = 0, 1, 2, 3, 7, 8, 9, 10, 11, 12
 SMALL = 16
+RELAY = 1
+TAKE = (8,)
 X_FIRST = (8, 4, 5, 6, 3, 0, 1, 2)
 Z_FIRST = (9, 10, 11, 7)
+SLOTS = (
+    ("x0", (0, 1, 2, 3, 4, 5, 6, 7)),
+    ("z0", (0, 2, 4, 6)),
+    ("x1", (1, 2, 3, 4, 5, 6, 7, 8)),
+    ("z1", (1, 3, 5, 7)),
+    ("x2", (2, 3, 4, 5, 6, 7, 8, 9)),
+    ("z2", (2, 4, 6, 8)),
+    ("x3", (3, 4, 5, 6, 7, 8, 9, 10)),
+    ("z3", (3, 5, 7, 9)),
+    ("x4", (4, 5, 6, 7, 8, 9, 10, 11)),
+)
+BESIDE = {"down": 0, "act": 0, "inner": 1, "up": 1, "attend": 2, "hidden": 3, "qkv": 3}
+SMALL_STEPS = (4, 5, 6, 8, 10)
+STEPS = 1 + max(max(steps) for _, steps in SLOTS)
 
 
 def dot(a, b):
@@ -93,10 +109,10 @@
     groups, depth, rs, seq = sizes
     (emb, token_grads, wq_in, wo_in, wu_in, wd_in, lens, scores, bias, gains, head_w,
      out_sec, out_gin, out_q, out_o, out_u, out_d, out_small,
-     big, s1, xr, zr, zw, xw, fin, peers,
+     big, rb, s1, xr, zr, zw, xw, fin, peers,
      hbuf, qkv, probs, mixed, n1, r1, first_low, act, gp, n2, r2, outb, gbuf, high, dd, da, dm, dqkv,
      small, sm_sib, sm_grp, sm_dp, sm_sec,
-     local_sem, io_sem, g_zr, g_xr, g_sr, g_send, y_send, y_recv,
+     local_sem, io_sem, g_zr, g_xr, g_sr, g_send, b_own, b_zr, b_xr, b_back, b_send, y_send, y_recv,
      r_send, r_sib, r_x, r_z, r_grp, r_fin, r_peer, sm_send, sm_recv) = refs
     stages = depth.bit_length() - 1
     pairs = 2
@@ -183,6 +199,53 @@
     def beside(m, zz, half):
         part = region(m, zz, half)
         return rcopy(part, part, g_send.at[2], g_sr.at[m], sibling)
+
+    def relayed(b, zz, half):
+        return rb.at[b, zz, :, span(half, HALF)]
+
+    def lend(b):
+        return rcopy(
+            region(CHUNKS - RELAY + b, z, par), relayed(b, z, par), b_send.at[0], b_own.at[b], other
+        )
+
+    def relay_along(b, zz, t):
+        part = relayed(b, zz, par)
+        return rcopy(part, part, b_send.at[1], b_zr.at[b, zz], dev(z_=flip(z, far[t])))
+
+    def relay_over(b, zz, half):
+        part = relayed(b, zz, half)
+        return rcopy(part, part, b_send.at[2], b_xr.at[b, zz], across)
+
+    def give_back(b, zz, half):
+        return rcopy(
+            relayed(b, zz, half), region(CHUNKS - RELAY + b, zz, half), b_send.at[3], b_back.at[b], other
+        )
+
+    def relay_own(b):
+        lend(b).wait_recv()
+        relay_along(b, z, 0).start()
+
+    def relay_arrived(t, b):
+        for mask in held[t]:
+            zz = flip(z, far[t] ^ mask)
+            relay_along(b, zz, t).wait_recv()
+            relay_over(b, zz, par).start()
+            give_back(b, zz, par).start()
+        if t + 1 < stages:
+            for mask in held[t + 1]:
+                relay_along(b, flip(z, mask), t + 1).start()
+
+    def relay_crossed(t, b):
+        for mask in held[t]:
+            zz = flip(z, far[t] ^ mask)
+            relay_over(b, zz, 1 - par).wait_recv()
+            give_back(b, zz, 1 - par).start()
+
+    def take(b):
+        got = big.at[pl.ds(0, (depth - 1) * rs), :]
+        rcopy(got, got, b_send.at[3], b_back.at[b], other).wait_recv()
+        for k in range(1, depth):
+            beside(CHUNKS - RELAY + b, (z + k) % depth, None).start()
 
     def bias_row(start, width=D):
         return bias[:, pl.ds(start, width)]
@@ -307,20 +370,39 @@
         both_pairs(lambda p: widen(p, k))
 
     plan = [early(k, functools.partial(early_project, k)) for k in range(3)]
-    plan.append(early(3, lambda: attend(0)))
-    plan.append(early(4, lambda: attend(1)))
-    plan.append(early(5, early_join))
-    plan += [early(5 + k, functools.partial(early_widen, k)) for k in range(4)]
-
-    @pl.loop(0, CHUNKS + stages + 1)
+    plan.append(early(2, lambda: attend(0)))
+    plan.append(early(3, lambda: attend(1)))
+    plan.append(early(4, early_join))
+    plan += [early(4 + k, functools.partial(early_widen, k)) for k in range(4)]
+
+    mine = jnp.where(first_section, CHUNKS - RELAY, CHUNKS)
+
+    @pl.loop(0, mine + stages + 1)
     def _(n):
-        pl.when(n < CHUNKS)(functools.partial(own_step, n))
+        pl.when(n < mine)(functools.partial(own_step, n))
+
+        @pl.when(first_section & (n < RELAY))
+        def _():
+            lend(n).start()
+            beside(CHUNKS - RELAY + n, z, None).start()
+
+        relay_stages = [relay_own]
+        for t in range(stages):
+            relay_stages.append(functools.partial(relay_arrived, t))
+        for lag, stage in enumerate(relay_stages):
+            b = n - 1 - lag
+            pl.when(~first_section & (b >= 0) & (b < RELAY))(functools.partial(stage, b))
+        for t in range(stages):
+            b = n - 3 - t
+            pl.when(~first_section & (b >= 0) & (b < RELAY))(functools.partial(relay_crossed, t, b))
         for t in range(stages):
             m = n - t - 1
-            pl.when((m >= 0) & (m < CHUNKS))(functools.partial(arrived, m, t))
+            pl.when((m >= 0) & (m < mine))(functools.partial(arrived, m, t))
         for t in range(stages):
             m = n - t - 2
-            pl.when((m >= 0) & (m < CHUNKS))(functools.partial(crossed, m, t))
+            pl.when((m >= 0) & (m < mine))(functools.partial(crossed, m, t))
+        for b in range(RELAY):
+            pl.when(first_section & (n == TAKE[b]))(functools.partial(take, b))
         for run in plan:
             run(n)
 
@@ -352,10 +434,28 @@
 
     pltpu.make_async_copy(outb, out_sec, io_sem.at[0]).start()
 
-    sent = big.at[pl.ds(0, CHUNKS * (depth - 1) * rs), pl.ds(0, HALF)]
-    rcopy(sent, sent, g_send.at[0], g_zr.at[0, 0], across).wait_send()
-    sent = big.at[pl.ds(0, CHUNKS * (depth - 1) * rs), pl.ds(0, HALF)]
-    rcopy(sent, sent, g_send.at[1], g_xr.at[0, 0], across).wait_send()
+    for is_first, count in ((first_section, CHUNKS - RELAY), (~first_section, CHUNKS)):
+
+        @pl.when(is_first)
+        def _(count=count):
+            sent = big.at[pl.ds(0, count * (depth - 1) * rs), pl.ds(0, HALF)]
+            rcopy(sent, sent, g_send.at[0], g_zr.at[0, 0], across).wait_send()
+            rcopy(sent, sent, g_send.at[1], g_xr.at[0, 0], across).wait_send()
+
+    def relay_sent(k, rows, cols):
+        sent = big.at[pl.ds(0, rows), pl.ds(0, cols)]
+        rcopy(sent, sent, b_send.at[k], b_own.at[0], other).wait_send()
+
+    @pl.when(first_section)
+    def _():
+        relay_sent(0, RELAY * rs, HALF)
+
+    @pl.when(~first_section)
+    def _():
+        relay_sent(1, RELAY * (depth - 1) * rs, HALF)
+        relay_sent(2, RELAY * (depth - 1) * rs, HALF)
+        relay_sent(3, RELAY * (depth - 1) * rs, D)
+
     sent = big.at[pl.ds(0, CHUNKS * depth * rs), :]
     rcopy(sent, sent, g_send.at[2], g_sr.at[0], sibling).wait_send()
 
@@ -464,21 +564,17 @@
         def _(m):
             sib_send(m)
 
-    def make_up():
-        @pl.loop(0, 4)
-        def _(k):
-            weight_grad(first_low, 0, gp, k * D, (4 + k) * D)
-            sib_send(4 + k)
+    def make_up(k):
+        weight_grad(first_low, 0, gp, k * D, (4 + k) * D)
+        sib_send(4 + k)
 
     def make_attn():
         weight_grad(mixed, 0, da, 0, 3 * D)
         sib_send(3)
 
-    def make_qkv():
-        @pl.loop(0, 3)
-        def _(k):
-            weight_grad(hbuf, 0, dqkv, k * D, k * D)
-            sib_send(k)
+    def make_qkv(k):
+        weight_grad(hbuf, 0, dqkv, k * D, k * D)
+        sib_send(k)
 
     def pair_sums(m):
         rcopy(s1.at[m], s1.at[m], r_send.at[0], r_sib.at[m], sibling).wait_recv()
@@ -506,28 +602,16 @@
             part[zz] = (part[zz].astype(F32) + landing[slots[t] + k].astype(F32)).astype(BF)
 
     def put_out(m):
-        for h in range(2):
-
-            def put(to, row, col, h=h):
+        def put(to, row, col):
+            for h in range(2):
                 rows = pl.ds(pl.multiple_of(row, 16), rs)
                 cols = pl.ds(pl.multiple_of(col + h * HALF, 128), HALF)
                 pltpu.make_async_copy(fin.at[m, h], to.at[rows, cols], io_sem.at[2]).start()
 
-            @pl.when(m >= 8)
-            def _(put=put):
-                put(out_d, (m - 8) * rs, 0)
-
-            @pl.when((m >= 4) & (m < 8))
-            def _(put=put):
-                put(out_u, 0, (m - 4) * D)
-
-            @pl.when(m == 3)
-            def _(put=put):
-                put(out_o, 0, 0)
-
-            @pl.when(m < 3)
-            def _(put=put):
-                put(out_q, 0, m * D)
+        pl.when(m >= 8)(lambda: put(out_d, (m - 8) * rs, 0))
+        pl.when((m >= 4) & (m < 8))(lambda: put(out_u, 0, (m - 4) * D))
+        pl.when(m == 3)(lambda: put(out_o, 0, 0))
+        pl.when(m < 3)(lambda: put(out_q, 0, m * D))
 
     def x_copy(q, m):
         return rcopy(
@@ -551,10 +635,15 @@
 
         line_send(xr.at[q], zr.at[q], m, 0, r_send.at[2])
 
-    def x_line(t, q, m):
-        line_add(xr.at[q], zr.at[q], m, t, r_send.at[2])
-        if t + 1 < stages:
-            line_send(xr.at[q], zr.at[q], m, t + 1, r_send.at[2])
+    def lines(part, landing, m, ts, send):
+        for t in ts:
+            line_add(part, landing, m, t, send)
+            if t + 1 < stages:
+                line_send(part, landing, m, t + 1, send)
+
+    def x_line(ts, q, m):
+        lines(xr.at[q], zr.at[q], m, ts, r_send.at[2])
+        if stages - 1 not in ts:
             return
         total = xr[q, z]
         if groups > 2:
@@ -582,10 +671,9 @@
         pair_sums(m)
         line_send(s1.at[m], zw.at[q], m, 0, r_send.at[3])
 
-    def z_line(t, q, m):
-        line_add(s1.at[m], zw.at[q], m, t, r_send.at[3])
-        if t + 1 < stages:
-            line_send(s1.at[m], zw.at[q], m, t + 1, r_send.at[3])
+    def z_line(ts, q, m):
+        lines(s1.at[m], zw.at[q], m, ts, r_send.at[3])
+        if stages - 1 not in ts:
             return
         xw[q, g] = s1[m, z]
         for k in range(1, groups):
@@ -603,24 +691,13 @@
         fin[m, 1] = total[:, HALF:]
         put_out(m)
 
-    x_stages = [x_start, x_halves] + [functools.partial(x_line, t) for t in range(stages)] + [x_finish]
-    z_stages = [z_start] + [functools.partial(z_line, t) for t in range(stages)] + [z_finish]
-    steps = max(len(X_FIRST) + len(x_stages), 2 * len(Z_FIRST) - 1 + len(z_stages)) - 1
-
-    def sum_step(i):
-        for lag in range(max(len(x_stages), len(z_stages))):
-            if lag < len(x_stages):
-
-                @pl.when((i >= lag) & (i < len(X_FIRST) + lag))
-                def _(lag=lag):
-                    x_stages[lag](i - lag, pick(i - lag, X_FIRST))
-
-            if lag < len(z_stages):
-
-                @pl.when((i >= lag) & (i < 2 * len(Z_FIRST) + lag) & ((i - lag) % 2 == 0))
-                def _(lag=lag):
-                    q = (i - lag) // 2
-                    z_stages[lag](q, pick(q, Z_FIRST))
+    first_line, last_lines = range(0, 1), range(1, stages)
+    if stages == 1:
+        first_line, last_lines = range(0, 0), range(0, 1)
+    x_stages = [
+        x_start, x_halves, functools.partial(x_line, first_line), functools.partial(x_line, last_lines), x_finish
+    ]
+    z_stages = [z_start, functools.partial(z_line, first_line), functools.partial(z_line, last_lines), z_finish]
 
     pltpu.make_async_copy(outb, out_sec, io_sem.at[0]).wait()
 
@@ -628,53 +705,23 @@
     def _():
         rcopy(outb, outb, y_send.at[0], y_recv.at[0], other).wait_send()
 
-    @pl.loop(0, pairs)
+    last = pairs - 1
+
+    @pl.loop(0, jnp.where(first_section, last, pairs))
     def _(p):
-        start_sums = first_section & (p == pairs - 1)
-
         @pl.when(first_section)
         def _():
             grad_copy(p).wait_recv()
 
         outer_norm(p)
-        pl.when(start_sums)(make_down)
         act_back(p)
-
-        @pl.when(start_sums)
-        def _():
-            sum_step(0)
-
         inner_norm(p)
-
-        @pl.when(start_sums)
-        def _():
-            make_up()
-            sum_step(1)
-
         attend_back(p)
-
-        @pl.when(start_sums)
-        def _():
-            sum_step(2)
-
         hidden_back(p)
 
         @pl.when(~first_section)
         def _():
             grad_copy(p).start()
-
-    pltpu.make_async_copy(high, out_gin, io_sem.at[1]).start()
-
-    @pl.when(~first_section)
-    def _():
-        make_down()
-        sum_step(0)
-        make_up()
-        sum_step(1)
-        sum_step(2)
-
-    make_attn()
-    make_qkv()
 
     def sm_copy(src, dst, recv, to):
         return rcopy(src, dst, sm_send.at[0], recv, to)
@@ -725,11 +772,54 @@
         def _():
             head_copy().wait_send()
 
-    @pl.loop(3, steps)
+    def make_inner():
+        @pl.loop(0, 4)
+        def _(k):
+            make_up(k)
+
+    def make_outer():
+        make_attn()
+
+        @pl.loop(0, 3)
+        def _(k):
+            make_qkv(k)
+
+        pltpu.make_async_copy(high, out_gin, io_sem.at[1]).start()
+
+    beside = (
+        ("down", make_down, False),
+        ("act", act_back, True),
+        ("inner", inner_norm, True),
+        ("up", make_inner, False),
+        ("attend", attend_back, True),
+        ("hidden", hidden_back, True),
+        ("qkv", make_outer, False),
+    )
+    smalls = (small_sib, small_grp, small_dp, small_sec, small_head)
+
+    @pl.when(first_section)
+    def _():
+        grad_copy(last).wait_recv()
+        outer_norm(last)
+
+    @pl.loop(0, STEPS)
     def _(i):
-        for at, part in ((3, small_sib), (4, small_grp), (5, small_dp), (6, small_sec), (8, small_head)):
-            pl.when(i == at)(part)
-        sum_step(i)
+        for name, part, inside in beside:
+            if inside:
+                pl.when(first_section & (i == BESIDE[name]))(functools.partial(part, last))
+            else:
+                pl.when(i == BESIDE[name])(part)
+        for step, part in zip(SMALL_STEPS, smalls):
+            pl.when(i == step)(part)
+        for name, at in SLOTS:
+            chunks, parts = (X_FIRST, x_stages) if name[0] == "x" else (Z_FIRST, z_stages)
+            q = jnp.int32(-1)
+            for k, step in enumerate(at):
+                q = jnp.where(i == step, k, q)
+
+            @pl.when(q >= 0)
+            def _(q=q, chunks=chunks, part=parts[int(name[1])]):
+                part(q, pick(q, chunks))
 
     count = 1 + (groups - 1) + (depth - 1)
     sent = high.at[pl.ds(0, count * SMALL), :]
@@ -776,6 +866,7 @@
     nx, nz = len(X_FIRST), len(Z_FIRST)
     scratch = [
         pltpu.VMEM((CHUNKS * D + FF, D), BF),
+        pltpu.VMEM((RELAY, depth, rs, D), BF),
         pltpu.VMEM((CHUNKS, depth, rs, D), BF),
         pltpu.VMEM((nx, depth, rs, HALF), BF),
         pltpu.VMEM((nx, max(depth - 1, 1), rs, HALF), BF),
@@ -812,6 +903,11 @@
         pltpu.SemaphoreType.DMA((CHUNKS, depth)),
         pltpu.SemaphoreType.DMA((CHUNKS,)),
         pltpu.SemaphoreType.DMA((3,)),
+        pltpu.SemaphoreType.DMA((RELAY,)),
+        pltpu.SemaphoreType.DMA((RELAY, depth)),
+        pltpu.SemaphoreType.DMA((RELAY, depth)),
+        pltpu.SemaphoreType.DMA((RELAY,)),
+        pltpu.SemaphoreType.DMA((4,)),
         pltpu.SemaphoreType.DMA((2,)),
         pltpu.SemaphoreType.DMA((4,)),
         pltpu.SemaphoreType.DMA((7,)),

time: 238 us -> 232 us (0.975)
  Pallas kernels: 237 us -> 231 us
    pallas_call x1, Pallas kernels: 232 us -> 226 us  [on_device(): pl.pallas_call(functools.partial(kernel, (groups, depth, rs, seq)), out_s...]
where the time goes in v3:
time: 232 us
  Pallas kernels  231 us (100%)
    pallas_call x1, Pallas kernels, on_device(): pl.pallas_call(functools.partial(kernel, (groups, depth, rs, seq)), out_s...  226 us
    pallas_call x1, Pallas kernels, on_device(): pl.pallas_call(hand_out, out_shape=[jax.ShapeDtypeStruct(x.shape, x.dtype...  4.81 us

profile of v3, /device:TPU:0, one launch (start us, length us, event | category | flops | bytes accessed | tf_op | source)
XLA Modules:
  0.0 231.5 jit_solution(7120220870775410236)
XLA Ops:
  0.6 226.1 %shard_map.178 = (bf16[512,768]{1,0:T(8,128)(2,1)}, f32[512,768]{1,0:T(8,128)}, bf16[96,2304]{1,0:T(8,128)(2,1)}, bf16[96,768]{1,0:T(8,128)(2,1)}, bf16[96,3072]...) custom-call(bf16[512,768]{1,0:T(8,128)(2,1)} %bitcast.20, bf16[512,768]{1,0:T(8,128)(2,1)} %bitcast.21, ...), custom_call_target="tpu_custom_call" | custom-call | tf_op jit(solution)/shard_map/pallas_call | solution.py:923
  226.7 4.8 %shard_map.179 = (bf16[512,768]{1,0:T(8,128)(2,1)}, f32[512,768]{1,0:T(8,128)}, f32[96,2304]{1,0:T(8,128)}, f32[96,768]{1,0:T(8,128)}, f32[96,3072]{1,0:T(8,128)...) custom-call(bf16[512,768]{1,0:T(8,128)(2,1)} %get-tuple-element.25.state, ...), custom_call_target="tpu_custom_call" | custom-call | tf_op jit(solution)/shard_map/pallas_call | solution.py:945

commit v4 on v3

--- a/solution.py
+++ b/solution.py
@@ -25,20 +25,20 @@
 SMALL = 16
 RELAY = 1
 TAKE = (8,)
-X_FIRST = (8, 4, 5, 6, 3, 0, 1, 2)
-Z_FIRST = (9, 10, 11, 7)
+X_FIRST = (8, 4, 5, 6, 7, 3, 0, 1, 2)
+Z_FIRST = (9, 10, 11)
 SLOTS = (
-    ("x0", (0, 1, 2, 3, 4, 5, 6, 7)),
-    ("z0", (0, 2, 4, 6)),
-    ("x1", (1, 2, 3, 4, 5, 6, 7, 8)),
-    ("z1", (1, 3, 5, 7)),
-    ("x2", (2, 3, 4, 5, 6, 7, 8, 9)),
-    ("z2", (2, 4, 6, 8)),
-    ("x3", (3, 4, 5, 6, 7, 8, 9, 10)),
-    ("z3", (3, 5, 7, 9)),
-    ("x4", (4, 5, 6, 7, 8, 9, 10, 11)),
+    ("x0", (0, 2, 1, 4, 3, 6, 5, 7, 9)),
+    ("z0", (0, 3, 2)),
+    ("z3", (14, 15, 17)),
+    ("x4", (8, 12, 9, 13, 11, 14, 15, 16, 17)),
+    ("x3", (6, 9, 7, 11, 8, 12, 13, 14, 15)),
+    ("z2", (4, 11, 13)),
+    ("x2", (3, 6, 4, 8, 7, 9, 11, 12, 13)),
+    ("z1", (2, 5, 7)),
+    ("x1", (1, 3, 2, 5, 4, 7, 8, 10, 11)),
 )
-BESIDE = {"down": 0, "act": 0, "inner": 1, "up": 1, "attend": 2, "hidden": 3, "qkv": 3}
+BESIDE = {"down": 0, "act": 1, "inner": 1, "up": 1, "attend": 3, "hidden": 4, "qkv": 5}
 SMALL_STEPS = (4, 5, 6, 8, 10)
 STEPS = 1 + max(max(steps) for _, steps in SLOTS)
 
@@ -88,7 +88,7 @@
 
 def gelu_parts(x):
     t = 1.0 / (1.0 + (0.3275911 * math.sqrt(0.5)) * jnp.abs(x))
-    e = jnp.exp(-0.5 * x * x)
+    e = jnp.exp2((-0.5 * math.log2(math.e)) * (x * x))
     tail = t * (0.127414796 + t * (-0.142248368 + t * (0.7107068705 + t * (-0.7265760135 + t * 0.5307027145)))) * e
     phi = jnp.where(x >= 0, 1.0 - tail, tail)
     return x * phi, phi + x * (e * (1.0 / math.sqrt(2.0 * math.pi)))
@@ -109,7 +109,7 @@
     groups, depth, rs, seq = sizes
     (emb, token_grads, wq_in, wo_in, wu_in, wd_in, lens, scores, bias, gains, head_w,
      out_sec, out_gin, out_q, out_o, out_u, out_d, out_small,
-     big, rb, s1, xr, zr, zw, xw, fin, peers,
+     big, s1, xr, zr, zw, xw, fin, peers,
      hbuf, qkv, probs, mixed, n1, r1, first_low, act, gp, n2, r2, outb, gbuf, high, dd, da, dm, dqkv,
      small, sm_sib, sm_grp, sm_dp, sm_sec,
      local_sem, io_sem, g_zr, g_xr, g_sr, g_send, b_own, b_zr, b_xr, b_back, b_send, y_send, y_recv,
@@ -201,7 +201,7 @@
         return rcopy(part, part, g_send.at[2], g_sr.at[m], sibling)
 
     def relayed(b, zz, half):
-        return rb.at[b, zz, :, span(half, HALF)]
+        return dd.at[pl.ds(pl.multiple_of((b * depth + zz) * rs, 16), rs), span(half, HALF)]
 
     def lend(b):
         return rcopy(
@@ -266,21 +266,31 @@
             x = x + bias_row(0 if k == 0 else D)
         qkv[r, pl.ds(k * D, D)] = x.astype(BF)
 
+    def both_heads(x):
+        none = jnp.zeros_like(x)
+        return jnp.concatenate([jnp.where(low, x, none), jnp.where(low, none, x)], 0)
+
+    def ahead(make):
+        coming = make(0)
+        for j in range(HEADS // 2):
+            now, coming = coming, make(j + 1) if j + 1 < HEADS // 2 else None
+            yield j, now
+
     def attend(p):
         r = pair_rows(p)
         ok = key < lens[p]
-        for j in range(HEADS // 2):
-            q2 = qkv[r, pl.ds(j * 128, 128)]
-            k2 = qkv[r, pl.ds((j + 6) * 128, 128)]
-            v2 = qkv[r, pl.ds((j + 12) * 128, 128)]
-            none = jnp.zeros_like(q2)
-            both = jnp.concatenate([jnp.where(low, q2, none), jnp.where(low, none, q2)], 0)
-            sc = jnp.where(ok, dot_t(both, k2) * SCALE, -1e30)
+
+        def scores_of(j):
+            q2 = qkv[r, pl.ds(j * 128, 128)] * jnp.asarray(SCALE, BF)
+            return dot_t(both_heads(q2), qkv[r, pl.ds((j + 6) * 128, 128)])
+
+        for j, sc in ahead(scores_of):
+            sc = jnp.where(ok, sc, -1e30)
             e = jnp.exp(sc - jnp.max(sc, -1, keepdims=True))
             pr = (e * (1.0 / jnp.sum(e, -1, keepdims=True))).astype(BF)
             probs[p * HEADS + 2 * j] = pr[:seq]
             probs[p * HEADS + 2 * j + 1] = pr[seq:]
-            o = dot(pr, v2)
+            o = dot(pr, qkv[r, pl.ds((j + 12) * 128, 128)])
             mixed[r, pl.ds(j * 128, 128)] = jnp.where(low, o[:seq], o[seq:]).astype(BF)
 
     def join(p):
@@ -315,7 +325,11 @@
 
     def state_copy(p):
         r = pair_rows(p)
-        return rcopy(outb.at[r, :], hbuf.at[r, :], y_send.at[0], y_recv.at[p], other)
+        return rcopy(outb.at[r, :], hbuf.at[r, :], y_send.at[p], y_recv.at[p], other)
+
+    def out_copy(p):
+        r = pair_rows(p)
+        return pltpu.make_async_copy(outb.at[r, :], out_sec.at[r, :], io_sem.at[p])
 
     def chunk_ready(m):
         whole = big.at[pl.ds(0, depth * rs), :]
@@ -416,23 +430,11 @@
         def _(p):
             narrow(p)
             state_copy(p).start()
+            out_copy(p).start()
 
     @pl.when(~first_section)
     def _():
         pltpu.make_async_copy(token_grads, gbuf, local_sem.at[1]).wait()
-
-        @pl.loop(0, pairs)
-        def _(p):
-            state_copy(p).wait_recv()
-            for k in range(3):
-                project(p, k)
-            attend(p)
-            join(p)
-            for k in range(4):
-                widen(p, k)
-            narrow(p)
-
-    pltpu.make_async_copy(outb, out_sec, io_sem.at[0]).start()
 
     for is_first, count in ((first_section, CHUNKS - RELAY), (~first_section, CHUNKS)):
 
@@ -503,20 +505,20 @@
 
     def attend_back(p):
         r = pair_rows(p)
-        for j in range(HEADS // 2):
+
+        def dprobs_of(j):
+            return dot_t(both_heads(dm[r, pl.ds(j * 128, 128)]), qkv[r, pl.ds((j + 12) * 128, 128)])
+
+        for j, dp in ahead(dprobs_of):
             q2 = qkv[r, pl.ds(j * 128, 128)]
             k2 = qkv[r, pl.ds((j + 6) * 128, 128)]
-            v2 = qkv[r, pl.ds((j + 12) * 128, 128)]
-            d2 = dm[r, pl.ds(j * 128, 128)]
-            none = jnp.zeros_like(d2)
-            both = jnp.concatenate([jnp.where(low, d2, none), jnp.where(low, none, d2)], 0)
             pr = jnp.concatenate([probs[p * HEADS + 2 * j], probs[p * HEADS + 2 * j + 1]], 0)
             pf = pr.astype(F32)
-            t = pf * dot_t(both, v2)
+            t = pf * dp
             ds = (t - pf * jnp.sum(t, -1, keepdims=True)).astype(BF)
             dq = dot(ds, k2)
             dq = (jnp.where(low, dq[:seq], dq[seq:]) * SCALE).astype(BF)
-            qt, dt = q2.T, d2.T
+            qt, dt = q2.T, dm[r, pl.ds(j * 128, 128)].T
             dk = jnp.concatenate([dot(qt[:HEAD], ds[:seq]), dot(qt[HEAD:], ds[seq:])], 0)
             dv = jnp.concatenate([dot(dt[:HEAD], pr[:seq]), dot(dt[HEAD:], pr[seq:])], 0)
             dk = (dk * SCALE).astype(BF).T
@@ -537,7 +539,7 @@
 
     def grad_copy(p):
         r = pair_rows(p)
-        return rcopy(outb.at[r, :], gbuf.at[r, :], y_send.at[1], y_recv.at[2 + p], other)
+        return rcopy(outb.at[r, :], gbuf.at[r, :], y_send.at[2 + p], y_recv.at[2 + p], other)
 
     def weight_grad(left, lcol, right, rcol, row):
         a = left[:, pl.ds(pl.multiple_of(lcol, 256), D)]
@@ -555,10 +557,19 @@
         def _(zz):
             sib_copy(m, zz).start()
 
-    def make_down():
+    def half_down(p):
+        r = pair_rows(p)
+
         @pl.loop(0, 4)
         def _(k):
-            weight_grad(act, k * D, dd, 0, DOWN_GRAD + k * D)
+            x = dot_c(act[r, span(k, D)], dd[r, :])
+            place = pl.ds(pl.multiple_of(DOWN_GRAD + k * D, 256), D)
+            if p > 0:
+                x = x + big[place, :].astype(F32)
+            big[place, :] = x.astype(BF)
+
+    def make_down():
+        half_down(last)
 
         @pl.loop(8, 12)
         def _(m):
@@ -606,7 +617,7 @@
             for h in range(2):
                 rows = pl.ds(pl.multiple_of(row, 16), rs)
                 cols = pl.ds(pl.multiple_of(col + h * HALF, 128), HALF)
-                pltpu.make_async_copy(fin.at[m, h], to.at[rows, cols], io_sem.at[2]).start()
+                pltpu.make_async_copy(fin.at[m, h], to.at[rows, cols], io_sem.at[3]).start()
 
         pl.when(m >= 8)(lambda: put(out_d, (m - 8) * rs, 0))
         pl.when((m >= 4) & (m < 8))(lambda: put(out_u, 0, (m - 4) * D))
@@ -699,16 +710,31 @@
     ]
     z_stages = [z_start, functools.partial(z_line, first_line), functools.partial(z_line, last_lines), z_finish]
 
-    pltpu.make_async_copy(outb, out_sec, io_sem.at[0]).wait()
-
-    @pl.when(first_section)
-    def _():
-        rcopy(outb, outb, y_send.at[0], y_recv.at[0], other).wait_send()
-
     last = pairs - 1
+
+    def hidden_step(p):
+        out_copy(p).wait()
+
+        @pl.when(first_section)
+        def _():
+            state_copy(p).wait_send()
+
+        hidden_back(p)
 
     @pl.loop(0, jnp.where(first_section, last, pairs))
     def _(p):
+        @pl.when(~first_section)
+        def _():
+            state_copy(p).wait_recv()
+            for k in range(3):
+                project(p, k)
+            attend(p)
+            join(p)
+            for k in range(4):
+                widen(p, k)
+            narrow(p)
+            out_copy(p).start()
+
         @pl.when(first_section)
         def _():
             grad_copy(p).wait_recv()
@@ -717,7 +743,7 @@
         act_back(p)
         inner_norm(p)
         attend_back(p)
-        hidden_back(p)
+        hidden_step(p)
 
         @pl.when(~first_section)
         def _():
@@ -784,7 +810,7 @@
         def _(k):
             make_qkv(k)
 
-        pltpu.make_async_copy(high, out_gin, io_sem.at[1]).start()
+        pltpu.make_async_copy(high, out_gin, io_sem.at[2]).start()
 
     beside = (
         ("down", make_down, False),
@@ -792,10 +818,13 @@
         ("inner", inner_norm, True),
         ("up", make_inner, False),
         ("attend", attend_back, True),
-        ("hidden", hidden_back, True),
+        ("hidden", hidden_step, True),
         ("qkv", make_outer, False),
     )
     smalls = (small_sib, small_grp, small_dp, small_sec, small_head)
+
+    for p in range(last):
+        half_down(p)
 
     @pl.when(first_section)
     def _():
@@ -827,10 +856,11 @@
 
     @pl.when(~first_section)
     def _():
-        rcopy(outb, outb, y_send.at[1], y_recv.at[0], other).wait_send()
-
-    pltpu.make_async_copy(high, out_gin, io_sem.at[1]).wait()
-    pltpu.make_async_copy(fin, fin, io_sem.at[2]).wait()
+        for p in range(pairs):
+            grad_copy(p).wait_send()
+
+    pltpu.make_async_copy(high, out_gin, io_sem.at[2]).wait()
+    pltpu.make_async_copy(fin, fin, io_sem.at[3]).wait()
     rcopy(s1, s1, r_send.at[0], r_sib.at[0], sibling).wait_send()
     rcopy(xr, xr, r_send.at[1], r_x.at[0], across).wait_send()
     if stages:
@@ -866,7 +896,6 @@
     nx, nz = len(X_FIRST), len(Z_FIRST)
     scratch = [
         pltpu.VMEM((CHUNKS * D + FF, D), BF),
-        pltpu.VMEM((RELAY, depth, rs, D), BF),
         pltpu.VMEM((CHUNKS, depth, rs, D), BF),
         pltpu.VMEM((nx, depth, rs, HALF), BF),
         pltpu.VMEM((nx, max(depth - 1, 1), rs, HALF), BF),
@@ -898,7 +927,7 @@
         pltpu.VMEM((depth, SMALL, D), F32),
         pltpu.VMEM((SMALL, D), F32),
         pltpu.SemaphoreType.DMA((2,)),
-        pltpu.SemaphoreType.DMA((3,)),
+        pltpu.SemaphoreType.DMA((4,)),
         pltpu.SemaphoreType.DMA((CHUNKS, depth)),
         pltpu.SemaphoreType.DMA((CHUNKS, depth)),
         pltpu.SemaphoreType.DMA((CHUNKS,)),
@@ -908,7 +937,7 @@
         pltpu.SemaphoreType.DMA((RELAY, depth)),
         pltpu.SemaphoreType.DMA((RELAY,)),
         pltpu.SemaphoreType.DMA((4,)),
-        pltpu.SemaphoreType.DMA((2,)),
+        pltpu.SemaphoreType.DMA((4,)),
         pltpu.SemaphoreType.DMA((4,)),
         pltpu.SemaphoreType.DMA((7,)),
         pltpu.SemaphoreType.DMA((CHUNKS,)),
@@ -927,7 +956,7 @@
         out_specs=(hbm,) * 6 + (vmem,),
         scratch_shapes=scratch,
         compiler_params=pltpu.CompilerParams(
-            collective_id=0, has_side_effects=True, vmem_limit_bytes=63 * 1024 * 1024
+            collective_id=0, has_side_effects=True, vmem_limit_bytes=65300 * 1024
         ),
     )(
         embedded.reshape(tokens, D),

time: 232 us -> 224 us (0.966)
  Pallas kernels: 231 us -> 224 us
    pallas_call x1, Pallas kernels: 226 us -> 219 us  [on_device(): pl.pallas_call(functools.partial(kernel, (groups, depth, rs, seq)), out_s...]
where the time goes in v4:
time: 224 us
  Pallas kernels  224 us (100%)
    pallas_call x1, Pallas kernels, on_device(): pl.pallas_call(functools.partial(kernel, (groups, depth, rs, seq)), out_s...  219 us
    pallas_call x1, Pallas kernels, on_device(): pl.pallas_call(hand_out, out_shape=[jax.ShapeDtypeStruct(x.shape, x.dtype...  4.81 us

profile of v4, /device:TPU:0, one launch (start us, length us, event | category | flops | bytes accessed | tf_op | source)
XLA Modules:
  0.0 224.2 jit_solution(9483219236638012178)
XLA Ops:
  0.6 218.7 %shard_map.178 = (bf16[512,768]{1,0:T(8,128)(2,1)}, f32[512,768]{1,0:T(8,128)}, bf16[96,2304]{1,0:T(8,128)(2,1)}, bf16[96,768]{1,0:T(8,128)(2,1)}, bf16[96,3072]...) custom-call(bf16[512,768]{1,0:T(8,128)(2,1)} %bitcast.20, bf16[512,768]{1,0:T(8,128)(2,1)} %bitcast.21, ...), custom_call_target="tpu_custom_call" | custom-call | tf_op jit(solution)/shard_map/pallas_call | solution.py:952
  219.4 4.8 %shard_map.179 = (bf16[512,768]{1,0:T(8,128)(2,1)}, f32[512,768]{1,0:T(8,128)}, f32[96,2304]{1,0:T(8,128)}, f32[96,768]{1,0:T(8,128)}, f32[96,3072]{1,0:T(8,128)...) custom-call(bf16[512,768]{1,0:T(8,128)(2,1)} %get-tuple-element.25.state, ...), custom_call_target="tpu_custom_call" | custom-call | tf_op jit(solution)/shard_map/pallas_call | solution.py:974

commit v5 on v4

--- a/solution.py
+++ b/solution.py
@@ -40,7 +40,10 @@
 )
 BESIDE = {"down": 0, "act": 1, "inner": 1, "up": 1, "attend": 3, "hidden": 4, "qkv": 5}
 SMALL_STEPS = (4, 5, 6, 8, 10)
-STEPS = 1 + max(max(steps) for _, steps in SLOTS)
+LENT = 4
+LENT_STEPS = (7, 9, 11, 13)
+LENT_BACK = 17
+STEPS = 1 + max(LENT_BACK, max(max(steps) for _, steps in SLOTS))
 
 
 def dot(a, b):
@@ -109,12 +112,13 @@
     groups, depth, rs, seq = sizes
     (emb, token_grads, wq_in, wo_in, wu_in, wd_in, lens, scores, bias, gains, head_w,
      out_sec, out_gin, out_q, out_o, out_u, out_d, out_small,
-     big, s1, xr, zr, zw, xw, fin, peers,
-     hbuf, qkv, probs, mixed, n1, r1, first_low, act, gp, n2, r2, outb, gbuf, high, dd, da, dm, dqkv,
+     big, s1, xr, zr, zw, xw, fin, peers, rz, rg,
+     hbuf, qkv, probs, mixed, n1, r1, first_low, act, gp, n2, r2, outb, gbuf, high, dd, dqkv,
      small, sm_sib, sm_grp, sm_dp, sm_sec,
-     local_sem, io_sem, g_zr, g_xr, g_sr, g_send, b_own, b_zr, b_xr, b_back, b_send, y_send, y_recv,
+     local_sem, io_sem, g_zr, g_xr, g_sr, g_send, b_own, b_zr, b_xr, b_back, b_send, k_in, k_z, k_g, k_out, k_send, y_send, y_recv,
      r_send, r_sib, r_x, r_z, r_grp, r_fin, r_peer, sm_send, sm_recv) = refs
     stages = depth.bit_length() - 1
+    da, dm = n1, n2
     pairs = 2
     sec = lax.axis_index("section")
     g = lax.axis_index("grp")
@@ -632,9 +636,66 @@
     def fin_copy(m):
         return rcopy(fin.at[m, par], fin.at[m, par], r_send.at[4], r_fin.at[m], across)
 
+    lent = X_FIRST[LENT]
+
+    def lent_shard(zz):
+        return qkv.at[pl.ds(pl.multiple_of(zz * rs, 16), rs), pl.ds(0, D)]
+
+    def lend_sums():
+        for zz in range(depth):
+            rcopy(s1.at[lent, zz], lent_shard(zz), k_send.at[0], k_in.at[0], other).start()
+
+    def lent_send(t):
+        for k, mask in enumerate(sides[t]):
+            rcopy(
+                lent_shard(flip(z, (1 << t) ^ mask)), rz.at[slots[t] + k], k_send.at[1], k_z.at[t],
+                dev(z_=flip(z, 1 << t)),
+            ).start()
+
+    def lent_add(t):
+        here = rz.at[pl.ds(slots[t], len(sides[t]))]
+        rcopy(here, here, k_send.at[1], k_z.at[t], dev(z_=flip(z, 1 << t))).wait_recv()
+        for k, mask in enumerate(sides[t]):
+            part = lent_shard(flip(z, mask))
+            part[...] = (part[...].astype(F32) + rz[slots[t] + k].astype(F32)).astype(BF)
+
+    def lent_start():
+        whole = qkv.at[pl.ds(0, depth * rs), pl.ds(0, D)]
+        rcopy(whole, whole, k_send.at[0], k_in.at[0], other).wait_recv()
+        lent_send(0)
+
+    def lent_line(ts):
+        for t in ts:
+            lent_add(t)
+            if t + 1 < stages:
+                lent_send(t + 1)
+        if stages - 1 in ts:
+            rg[g] = lent_shard(z)[...]
+            for k in range(1, groups):
+                rcopy(rg.at[g], rg.at[g], k_send.at[2], k_g.at[g], dev(g_=(g + k) % groups)).start()
+
+    def lent_done():
+        for k in range(1, groups):
+            gg = (g + k) % groups
+            rcopy(rg.at[gg], rg.at[gg], k_send.at[2], k_g.at[gg], across).wait_recv()
+        total = rg[0].astype(F32)
+        for k in range(1, groups):
+            total = total + rg[k].astype(F32)
+        qkv[pl.ds(0, rs), pl.ds(D, D)] = total.astype(BF)
+        for h in range(2):
+            rcopy(
+                qkv.at[pl.ds(0, rs), pl.ds(D + h * HALF, HALF)], fin.at[lent, h], k_send.at[3], k_out.at[0], other
+            ).start()
+
+    def lent_back():
+        rcopy(fin.at[lent], fin.at[lent], k_send.at[3], k_out.at[0], other).wait_recv()
+        put_out(jnp.int32(lent))
+
     def x_start(q, m):
         pair_sums(m)
-        x_copy(q, m).start()
+        lends = first_section & (q == LENT)
+        pl.when(lends)(lend_sums)
+        pl.when(~lends)(lambda: x_copy(q, m).start())
 
     def x_halves(q, m):
         x_copy(q, m).wait_recv()
@@ -821,6 +882,9 @@
         ("hidden", hidden_step, True),
         ("qkv", make_outer, False),
     )
+    lent_parts = (
+        lent_start, functools.partial(lent_line, first_line), functools.partial(lent_line, last_lines), lent_done
+    )
     smalls = (small_sib, small_grp, small_dp, small_sec, small_head)
 
     for p in range(last):
@@ -840,13 +904,20 @@
                 pl.when(i == BESIDE[name])(part)
         for step, part in zip(SMALL_STEPS, smalls):
             pl.when(i == step)(part)
+        for step, part in zip(LENT_STEPS, lent_parts):
+            pl.when(~first_section & (i == step))(part)
+        pl.when(first_section & (i == LENT_BACK))(lent_back)
         for name, at in SLOTS:
             chunks, parts = (X_FIRST, x_stages) if name[0] == "x" else (Z_FIRST, z_stages)
             q = jnp.int32(-1)
             for k, step in enumerate(at):
                 q = jnp.where(i == step, k, q)
 
-            @pl.when(q >= 0)
+            runs = q >= 0
+            if name[0] == "x" and name[1] != "0":
+                runs = runs & ~(first_section & (q == LENT))
+
+            @pl.when(runs)
             def _(q=q, chunks=chunks, part=parts[int(name[1])]):
                 part(q, pick(q, chunks))
 
@@ -862,15 +933,33 @@
     pltpu.make_async_copy(high, out_gin, io_sem.at[2]).wait()
     pltpu.make_async_copy(fin, fin, io_sem.at[3]).wait()
     rcopy(s1, s1, r_send.at[0], r_sib.at[0], sibling).wait_send()
-    rcopy(xr, xr, r_send.at[1], r_x.at[0], across).wait_send()
-    if stages:
-        rcopy(zr, zr, r_send.at[2], r_z.at[0, 0], across).wait_send()
-        rcopy(zw, zw, r_send.at[3], r_z.at[0, 0], across).wait_send()
-    part = fin.at[pl.ds(0, len(X_FIRST)), 0]
-    rcopy(part, part, r_send.at[4], r_fin.at[0], across).wait_send()
-    if groups > 2:
-        part = peers.at[:, pl.ds(0, groups // 2 - 1)]
-        rcopy(part, part, r_send.at[5], r_peer.at[0, 0], across).wait_send()
+    for is_here, chunks in ((first_section, len(X_FIRST) - 1), (~first_section, len(X_FIRST))):
+
+        @pl.when(is_here)
+        def _(chunks=chunks):
+            part = xr.at[pl.ds(0, chunks)]
+            rcopy(part, part, r_send.at[1], r_x.at[0], across).wait_send()
+            part = zr.at[pl.ds(0, chunks)]
+            rcopy(part, part, r_send.at[2], r_z.at[0, 0], across).wait_send()
+            part = fin.at[pl.ds(0, chunks), 0]
+            rcopy(part, part, r_send.at[4], r_fin.at[0], across).wait_send()
+            if groups > 2:
+                part = peers.at[pl.ds(0, chunks), pl.ds(0, groups // 2 - 1)]
+                rcopy(part, part, r_send.at[5], r_peer.at[0, 0], across).wait_send()
+
+    rcopy(zw, zw, r_send.at[3], r_z.at[0, 0], across).wait_send()
+
+    @pl.when(first_section)
+    def _():
+        rcopy(s1.at[0], s1.at[0], k_send.at[0], k_in.at[0], other).wait_send()
+
+    @pl.when(~first_section)
+    def _():
+        rcopy(rz, rz, k_send.at[1], k_z.at[0], across).wait_send()
+        part = rg.at[pl.ds(0, groups - 1)]
+        rcopy(part, part, k_send.at[2], k_g.at[0], across).wait_send()
+        rcopy(fin.at[0], fin.at[0], k_send.at[3], k_out.at[0], other).wait_send()
+
     part = xw.at[:, pl.ds(0, groups - 1)]
     rcopy(part, part, r_send.at[6], r_grp.at[0, 0], across).wait_send()
 
@@ -903,6 +992,8 @@
         pltpu.VMEM((nz, groups, rs, D), BF),
         pltpu.VMEM((CHUNKS, 2, rs, HALF), BF),
         pltpu.VMEM((nx, teams, rs, HALF) if groups > 2 else (1, 1, 16, 128), BF),
+        pltpu.VMEM((max(depth - 1, 1), rs, D), BF),
+        pltpu.VMEM((groups, rs, D), BF),
         pltpu.VMEM((tokens, D), BF),
         pltpu.VMEM((tokens, 3 * D), BF),
         pltpu.VMEM((micro * HEADS, seq, seq), BF),
@@ -917,8 +1008,6 @@
         pltpu.VMEM((tokens, D), BF),
         pltpu.VMEM((tokens, D), BF),
         pltpu.VMEM((tokens, D), F32),
-        pltpu.VMEM((tokens, D), BF),
-        pltpu.VMEM((tokens, D), BF),
         pltpu.VMEM((tokens, D), BF),
         pltpu.VMEM((tokens, 3 * D), BF),
         pltpu.VMEM((SMALL, D), F32),
@@ -936,6 +1025,11 @@
         pltpu.SemaphoreType.DMA((RELAY, depth)),
         pltpu.SemaphoreType.DMA((RELAY, depth)),
         pltpu.SemaphoreType.DMA((RELAY,)),
+        pltpu.SemaphoreType.DMA((4,)),
+        pltpu.SemaphoreType.DMA((1,)),
+        pltpu.SemaphoreType.DMA((max(stages, 1),)),
+        pltpu.SemaphoreType.DMA((groups,)),
+        pltpu.SemaphoreType.DMA((1,)),
         pltpu.SemaphoreType.DMA((4,)),
         pltpu.SemaphoreType.DMA((4,)),
         pltpu.SemaphoreType.DMA((4,)),

time: 224 us -> 221 us (0.987)
  Pallas kernels: 224 us -> 219 us
    pallas_call x1, Pallas kernels: 219 us -> 215 us  [on_device(): pl.pallas_call(functools.partial(kernel, (groups, depth, rs, seq)), out_s...]
where the time goes in v5:
time: 221 us; the launch traced here: 220 us
  Pallas kernels  219 us (99%)
    pallas_call x1, Pallas kernels, on_device(): pl.pallas_call(functools.partial(kernel, (groups, depth, rs, seq)), out_s...  215 us
    pallas_call x1, Pallas kernels, on_device(): pl.pallas_call(hand_out, out_shape=[jax.ShapeDtypeStruct(x.shape, x.dtype...  4.81 us

profile of v5, /device:TPU:0, one launch (start us, length us, event | category | flops | bytes accessed | tf_op | source)
XLA Modules:
  0.0 220.0 jit_solution(11836073168834350264)
XLA Ops:
  0.6 214.6 %shard_map.178 = (bf16[512,768]{1,0:T(8,128)(2,1)}, f32[512,768]{1,0:T(8,128)}, bf16[96,2304]{1,0:T(8,128)(2,1)}, bf16[96,768]{1,0:T(8,128)(2,1)}, bf16[96,3072]...) custom-call(bf16[512,768]{1,0:T(8,128)(2,1)} %bitcast.20, bf16[512,768]{1,0:T(8,128)(2,1)} %bitcast.21, ...), custom_call_target="tpu_custom_call" | custom-call | tf_op jit(solution)/shard_map/pallas_call | solution.py:1046
  215.2 4.8 %shard_map.179 = (bf16[512,768]{1,0:T(8,128)(2,1)}, f32[512,768]{1,0:T(8,128)}, f32[96,2304]{1,0:T(8,128)}, f32[96,768]{1,0:T(8,128)}, f32[96,3072]{1,0:T(8,128)...) custom-call(bf16[512,768]{1,0:T(8,128)(2,1)} %get-tuple-element.25.state, ...), custom_call_target="tpu_custom_call" | custom-call | tf_op jit(solution)/shard_map/pallas_call | solution.py:1068

commit v6 on v5

--- a/solution.py
+++ b/solution.py
@@ -110,12 +110,12 @@
 
 def kernel(sizes, *refs):
     groups, depth, rs, seq = sizes
-    (emb, token_grads, wq_in, wo_in, wu_in, wd_in, lens, scores, bias, gains, head_w,
+    (emb, token_grads, wq_in, wo_in, wu_in, wd_in, bias_in, gains_in, head_in, lens, scores,
      out_sec, out_gin, out_q, out_o, out_u, out_d, out_small,
      big, s1, xr, zr, zw, xw, fin, peers, rz, rg,
      hbuf, qkv, probs, mixed, n1, r1, first_low, act, gp, n2, r2, outb, gbuf, high, dd, dqkv,
      small, sm_sib, sm_grp, sm_dp, sm_sec,
-     local_sem, io_sem, g_zr, g_xr, g_sr, g_send, b_own, b_zr, b_xr, b_back, b_send, k_in, k_z, k_g, k_out, k_send, y_send, y_recv,
+     bias, gains, head_w, local_sem, io_sem, g_zr, g_xr, g_sr, g_send, b_own, b_zr, b_xr, b_back, b_send, k_in, k_z, k_g, k_out, k_send, y_send, y_recv,
      r_send, r_sib, r_x, r_z, r_grp, r_fin, r_peer, sm_send, sm_recv) = refs
     stages = depth.bit_length() - 1
     da, dm = n1, n2
@@ -171,6 +171,17 @@
         wd_in, big.at[pl.ds(pl.multiple_of(DOWN + d * 4 * rs, 16), 4 * rs), :], local_sem.at[0]
     ).start()
 
+    vectors = [
+        pltpu.make_async_copy(src, dst, local_sem.at[2 + k])
+        for k, (src, dst) in enumerate(((bias_in, bias), (gains_in, gains), (head_in, head_w)))
+    ]
+    for copy in vectors:
+        copy.start()
+
+    def have_vectors():
+        for copy in vectors:
+            copy.wait()
+
     @pl.when(first_section)
     def _():
         pltpu.make_async_copy(emb, hbuf, local_sem.at[1]).start()
@@ -376,6 +387,7 @@
     def early_project(k):
         if k == 0:
             pltpu.make_async_copy(emb, hbuf, local_sem.at[1]).wait()
+            have_vectors()
         chunk_ready(k)
         both_pairs(lambda p: project(p, k))
 
@@ -439,6 +451,7 @@
     @pl.when(~first_section)
     def _():
         pltpu.make_async_copy(token_grads, gbuf, local_sem.at[1]).wait()
+        have_vectors()
 
     for is_first, count in ((first_section, CHUNKS - RELAY), (~first_section, CHUNKS)):
 
@@ -1015,7 +1028,10 @@
         pltpu.VMEM((groups, SMALL, D), F32),
         pltpu.VMEM((depth, SMALL, D), F32),
         pltpu.VMEM((SMALL, D), F32),
-        pltpu.SemaphoreType.DMA((2,)),
+        pltpu.VMEM(biases.shape, F32),
+        pltpu.VMEM(gains.shape[1:], F32),
+        pltpu.VMEM(head_weight.shape, F32),
+        pltpu.SemaphoreType.DMA((5,)),
         pltpu.SemaphoreType.DMA((4,)),
         pltpu.SemaphoreType.DMA((CHUNKS, depth)),
         pltpu.SemaphoreType.DMA((CHUNKS, depth)),
@@ -1046,7 +1062,7 @@
     state, grad_in, *grads, small = pl.pallas_call(
         functools.partial(kernel, (groups, depth, rs, seq)),
         out_shape=out_shape,
-        in_specs=[hbm] * 6 + [smem] * 2 + [vmem] * 3,
+        in_specs=[hbm] * 9 + [smem] * 2,
         out_specs=(hbm,) * 6 + (vmem,),
         scratch_shapes=scratch,
         compiler_params=pltpu.CompilerParams(
@@ -1059,11 +1075,11 @@
         w_attn_out[0],
         w_up[0],
         w_down[0],
-        lengths.reshape(micro),
-        score_grads.reshape(micro),
         biases,
         gains[0],
         head_weight,
+        lengths.reshape(micro),
+        score_grads.reshape(micro),
     )
     results = pl.pallas_call(
         hand_out,

time: 221 us -> 220 us (level)
  no operation moved by 1% of the time
where the time goes in v6:
time: 220 us
  Pallas kernels  219 us (100%)
    pallas_call x1, Pallas kernels, on_device(): pl.pallas_call(functools.partial(kernel, (groups, depth, rs, seq)), out_s...  215 us
    pallas_call x1, Pallas kernels, on_device(): pl.pallas_call(hand_out, out_shape=[jax.ShapeDtypeStruct(x.shape, x.dtype...  4.81 us

profile of v6, /device:TPU:0, one launch (start us, length us, event | category | flops | bytes accessed | tf_op | source)
XLA Modules:
  0.0 220.0 jit_solution(10085380291829411101)
XLA Ops:
  0.6 214.6 %shard_map.178 = (bf16[512,768]{1,0:T(8,128)(2,1)}, f32[512,768]{1,0:T(8,128)}, bf16[96,2304]{1,0:T(8,128)(2,1)}, bf16[96,768]{1,0:T(8,128)(2,1)}, bf16[96,3072]...) custom-call(bf16[512,768]{1,0:T(8,128)(2,1)} %bitcast.20, bf16[512,768]{1,0:T(8,128)(2,1)} %bitcast.21, ...), custom_call_target="tpu_custom_call" | custom-call | tf_op jit(solution)/shard_map/pallas_call | solution.py:1062
  215.2 4.8 %shard_map.179 = (bf16[512,768]{1,0:T(8,128)(2,1)}, f32[512,768]{1,0:T(8,128)}, f32[96,2304]{1,0:T(8,128)}, f32[96,768]{1,0:T(8,128)}, f32[96,3072]{1,0:T(8,128)...) custom-call(bf16[512,768]{1,0:T(8,128)(2,1)} %get-tuple-element.25.state, ...), custom_call_target="tpu_custom_call" | custom-call | tf_op jit(solution)/shard_map/pallas_call | solution.py:1084

commit v7 on v6

--- a/solution.py
+++ b/solution.py
@@ -39,6 +39,7 @@
     ("x1", (1, 3, 2, 5, 4, 7, 8, 10, 11)),
 )
 BESIDE = {"down": 0, "act": 1, "inner": 1, "up": 1, "attend": 3, "hidden": 4, "qkv": 5}
+UP_ORDER = (1, 0, 3, 2)
 SMALL_STEPS = (4, 5, 6, 8, 10)
 LENT = 4
 LENT_STEPS = (7, 9, 11, 13)
@@ -872,19 +873,20 @@
         def _():
             head_copy().wait_send()
 
-    def make_inner():
-        @pl.loop(0, 4)
-        def _(k):
-            make_up(k)
-
-    def make_outer():
-        make_attn()
-
-        @pl.loop(0, 3)
-        def _(k):
-            make_qkv(k)
-
-        pltpu.make_async_copy(high, out_gin, io_sem.at[2]).start()
+    def make_inner(i):
+        make_up(pick(i - BESIDE["up"], UP_ORDER))
+
+    def make_outer(i):
+        at = i - BESIDE["qkv"]
+        pl.when(at == 1)(make_attn)
+
+        @pl.when(at != 1)
+        def _():
+            make_qkv(jnp.where(at == 0, 0, at - 1))
+
+        @pl.when(at == 0)
+        def _():
+            pltpu.make_async_copy(high, out_gin, io_sem.at[2]).start()
 
     beside = (
         ("down", make_down, False),
@@ -913,8 +915,10 @@
         for name, part, inside in beside:
             if inside:
                 pl.when(first_section & (i == BESIDE[name]))(functools.partial(part, last))
+            elif name == "down":
+                pl.when(i == BESIDE[name])(part)
             else:
-                pl.when(i == BESIDE[name])(part)
+                pl.when((i >= BESIDE[name]) & (i < BESIDE[name] + 4))(functools.partial(part, i))
         for step, part in zip(SMALL_STEPS, smalls):
             pl.when(i == step)(part)
         for step, part in zip(LENT_STEPS, lent_parts):

time: 220 us -> 223 us (1.014); the launches traced: 220 us -> 221 us
  no operation moved by 1% of the time
where the time goes in v7:
time: 223 us; the launch traced here: 221 us
  Pallas kernels  220 us (99%)
    pallas_call x1, Pallas kernels, on_device(): pl.pallas_call(functools.partial(kernel, (groups, depth, rs, seq)), out_s...  215 us
    pallas_call x1, Pallas kernels, on_device(): pl.pallas_call(hand_out, out_shape=[jax.ShapeDtypeStruct(x.shape, x.dtype...  4.81 us

profile of v7, /device:TPU:0, one launch (start us, length us, event | category | flops | bytes accessed | tf_op | source)
XLA Modules:
  0.0 220.5 jit_solution(1155477471868689926)
XLA Ops:
  0.6 215.1 %shard_map.178 = (bf16[512,768]{1,0:T(8,128)(2,1)}, f32[512,768]{1,0:T(8,128)}, bf16[96,2304]{1,0:T(8,128)(2,1)}, bf16[96,768]{1,0:T(8,128)(2,1)}, bf16[96,3072]...) custom-call(bf16[512,768]{1,0:T(8,128)(2,1)} %bitcast.20, bf16[512,768]{1,0:T(8,128)(2,1)} %bitcast.21, ...), custom_call_target="tpu_custom_call" | custom-call | tf_op jit(solution)/shard_map/pallas_call | solution.py:1066
  215.7 4.8 %shard_map.179 = (bf16[512,768]{1,0:T(8,128)(2,1)}, f32[512,768]{1,0:T(8,128)}, f32[96,2304]{1,0:T(8,128)}, f32[96,768]{1,0:T(8,128)}, f32[96,3072]{1,0:T(8,128)...) custom-call(bf16[512,768]{1,0:T(8,128)(2,1)} %get-tuple-element.25.state, ...), custom_call_target="tpu_custom_call" | custom-call | tf_op jit(solution)/shard_map/pallas_call | solution.py:1088
